TPU v7x, 768 devices: a whole 4x8x12 slice. The times are simulated.
768 devices in a mesh: seq: 96 (over x, z, core), head: 8 (over y).
Axes of the slice: x: 4, y: 8, z: 12, core: 2. Of those that a mesh axis runs over, the one named last changes fastest.
Arguments:
- queries: bfloat16 [12288, 16, 128], P('seq', 'head'), may hold values from -6 to 6
- keys: bfloat16 [12288, 16, 128], P('seq', 'head'), may hold values from -1.5 to 1.5
- values: bfloat16 [12288, 16, 128], P('seq', 'head'), may hold values from -6 to 6
- reg: float32 [16], P('head'), may hold values from 1 to 8
- steps: int32 [96, 16], P('seq', 'head'), may hold values from 1 to 12, as said below
- w_out: bfloat16 [2048, 2048], P('head'), may hold values from -0.125 to 0.125
- d_y: bfloat16 [12288, 2048], P(('seq', 'head')), may hold values from -6 to 6
Outputs:
- out: bfloat16 [12288, 2048], P(('seq', 'head'))
- grad_queries: bfloat16 [12288, 16, 128], P('seq', 'head')
- grad_keys: bfloat16 [12288, 16, 128], P('seq', 'head')
- grad_values: bfloat16 [12288, 16, 128], P('seq', 'head')
Inputs may be any that keep to these rules, and one draw needn't show every extreme that they name: steps[b, h] counts the conjugate-gradient steps of block b of 128 tokens and head h; some entry equals 12 in every draw.
All inputs are finite; a program needn't handle non-finite values.
Results may differ from a plain program's by a relative error of at most 0.022.
Values may be sent and summed in bfloat16 or wider, within the bound.
No kernel may reach another device: no remote copies, remote signals or barrier semaphores. Data moves between devices by JAX's collectives and lax.ppermute only.
A program may use at most 128 MiB of HBM per device.

v0:
```python
import jax
import jax.numpy as jnp
from jax import lax
from jax.sharding import PartitionSpec as P

STEPS_MAX = 12


epsilon = 1e-06
highest = lax.Precision.HIGHEST


def carried_in(value, axis, join, neutral):
    place = lax.axis_index(axis)
    gathered = jax.tree.map(
        lambda a, kind: lax.all_gather(a.astype(kind), axis), value, (jnp.bfloat16, jnp.bfloat16)
    )
    state = jax.tree.map(lambda a, e: jnp.zeros_like(a) + jnp.asarray(e, a.dtype), value, neutral)

    def carried_one(hop, state):
        return join(
            state,
            jax.tree.map(
                lambda a, own: lax.dynamic_index_in_dim(a, hop, 0, False).astype(own.dtype),
                gathered,
                value,
            ),
        )

    return lax.fori_loop(0, place, carried_one, state)


def prefix(value, axis, join, neutral):
    count = lax.axis_size(axis)
    place = lax.axis_index(axis)
    ahead = count - 1 - place
    gathered = jax.tree.map(
        lambda a, kind: lax.all_gather(a.astype(kind), axis),
        value,
        jax.tree.map(lambda a: jnp.bfloat16 if a.dtype == jnp.float32 else a.dtype, value),
    )
    state = jax.tree.map(lambda a, e: jnp.zeros_like(a) + jnp.asarray(e, a.dtype), value, neutral)

    def prefix_one(hop, state):
        source = count - 1 - hop
        return join(
            state,
            jax.tree.map(
                lambda a, own: lax.dynamic_index_in_dim(a, source, 0, False).astype(own.dtype),
                gathered,
                value,
            ),
        )

    return lax.fori_loop(0, ahead, prefix_one, state)


def apply_cov(direction, key_rows, cov_prev, ridge, causal_low):
    result = jnp.einsum("rhsd,hde->rhse", direction, cov_prev, precision=highest)
    scores = jnp.einsum("rhsd,htd->rhst", direction, key_rows, precision=highest) * causal_low
    result = result + jnp.einsum("rhst,htd->rhsd", scores, key_rows, precision=highest)
    return result + ridge[:, None, None] * direction


def cg_solve(right, key_rows, cov_prev, ridge, counts, causal_low):

    def cg_step(step_idx, cg_state):
        sol, resid, direction, resid_sq = cg_state
        image = apply_cov(direction, key_rows, cov_prev, ridge, causal_low)
        step_len = resid_sq / (jnp.sum(direction * image, -1, keepdims=True) + epsilon)
        sol_new = sol + step_len * direction
        resid_new = resid - step_len * image
        sq_new = jnp.sum(resid_new * resid_new, -1, keepdims=True)
        dir_new = resid_new + sq_new / (resid_sq + epsilon) * direction
        live_mask = (step_idx < counts)[:, None, None]
        return (
            jnp.where(live_mask, sol_new, sol),
            jnp.where(live_mask, resid_new, resid),
            jnp.where(live_mask, dir_new, direction),
            jnp.where(live_mask, sq_new, resid_sq),
        )

    start_state = (jnp.zeros_like(right), right, right, jnp.sum(right * right, -1, keepdims=True))
    return lax.fori_loop(0, STEPS_MAX, cg_step, start_state)[0]


def add_pairs(earlier, later):
    return (earlier[0] + later[0], earlier[1] + later[1])


def local(queries, keys, values, reg, steps, w_out, d_y):
    size_c = queries.shape[0]
    head_count = queries.shape[1]
    head_size = queries.shape[2]

    def heads_first(array):
        return jnp.transpose(array, (1, 0, 2)).astype(jnp.float32)

    query_h, key_h, value_h = (heads_first(queries), heads_first(keys), heads_first(values))
    counts = steps[0]
    positions = jnp.arange(size_c)
    causal_low = (positions[:, None] >= positions[None, :]).astype(jnp.float32)
    causal_up = (positions[:, None] <= positions[None, :]).astype(jnp.float32)
    zero_mats = jnp.zeros((head_count, head_size, head_size), jnp.float32)
    cov_own = jnp.einsum("hcd,hce->hde", key_h, key_h, precision=highest)
    state_own = jnp.einsum("hcv,hck->hvk", value_h, key_h, precision=highest)
    cov_prev, state_prev = carried_in(
        (cov_own, state_own), "seq", add_pairs, (zero_mats, zero_mats)
    )
    back_flat = lax.dot_general(
        lax.all_gather(d_y, "head", axis=0, tiled=True),
        w_out,
        (((1,), (1,)), ((), ())),
        preferred_element_type=jnp.float32,
    )
    back_h = jnp.transpose(back_flat.reshape(size_c, head_count, head_size), (1, 0, 2))
    scores_b = jnp.einsum("hcv,htv->hct", back_h, value_h, precision=highest) * causal_low
    adjoint = jnp.einsum("hcv,hvk->hck", back_h, state_prev, precision=highest)
    adjoint = adjoint + jnp.einsum("hct,htk->hck", scores_b, key_h, precision=highest)
    solved = cg_solve(jnp.stack([query_h, adjoint]), key_h, cov_prev, reg, counts, causal_low)
    sol = solved[0]
    dual = solved[1]
    scores = jnp.einsum("hck,htk->hct", sol, key_h, precision=highest) * causal_low
    mixed = jnp.einsum("hck,hvk->hcv", sol, state_prev, precision=highest)
    mixed = mixed + jnp.einsum("hct,htv->hcv", scores, value_h, precision=highest)
    mixed_flat = jnp.transpose(mixed.astype(jnp.bfloat16), (1, 0, 2)).reshape(
        size_c, head_count * head_size
    )
    out = lax.psum_scatter(
        jnp.dot(mixed_flat, w_out, preferred_element_type=jnp.float32).astype(jnp.bfloat16),
        "head",
        scatter_dimension=0,
        tiled=True,
    )
    outer_sum = jnp.einsum("hsd,hse->hde", dual, sol, precision=highest)
    sym_own = outer_sum + jnp.swapaxes(outer_sum, 1, 2)
    cross_own = jnp.einsum("hsv,hsk->hvk", back_h, sol, precision=highest)
    sym_sum, cross_sum = prefix((sym_own, cross_own), "seq", add_pairs, (zero_mats, zero_mats))
    m_one = jnp.einsum("hid,hsd->his", key_h, sol, precision=highest) * causal_up
    m_two = jnp.einsum("hid,hsd->his", key_h, dual, precision=highest) * causal_up
    m_three = jnp.einsum("hiv,hsv->his", value_h, back_h, precision=highest) * causal_up
    neg_part = jnp.einsum("hie,hde->hid", key_h, sym_sum, precision=highest)
    neg_part = neg_part + jnp.einsum("his,hsd->hid", m_one, dual, precision=highest)
    neg_part = neg_part + jnp.einsum("his,hsd->hid", m_two, sol, precision=highest)
    grad_k = jnp.einsum("hiv,hvk->hik", value_h, cross_sum, precision=highest)
    grad_k = grad_k + jnp.einsum("his,hsk->hik", m_three, sol, precision=highest) - neg_part
    grad_v = jnp.einsum("hik,hvk->hiv", key_h, cross_sum, precision=highest)
    grad_v = grad_v + jnp.einsum("his,hsv->hiv", m_one, back_h, precision=highest)
    grad_queries = jnp.transpose(dual, (1, 0, 2)).astype(jnp.bfloat16)
    grad_keys = jnp.transpose(grad_k.astype(jnp.bfloat16), (1, 0, 2))
    grad_values = jnp.transpose(grad_v.astype(jnp.bfloat16), (1, 0, 2))
    return (out, grad_queries, grad_keys, grad_values)


def solution(mesh):
    placed = (
        P("seq", "head", None),
        P("seq", "head", None),
        P("seq", "head", None),
        P("head"),
        P("seq", "head"),
        P("head", None),
        P(("seq", "head"), None),
    )
    return jax.shard_map(
        local,
        mesh=mesh,
        in_specs=placed,
        out_specs=(
            P(("seq", "head"), None),
            P("seq", "head", None),
            P("seq", "head", None),
            P("seq", "head", None),
        ),
        check_vma=False,
    )
```

profile of v0, /device:TPU:1, one launch (start us, length us, event | category | flops | bytes accessed | tf_op | source)
XLA Modules:
  0.0 706.6 jit_solution(7298310865605504555)
XLA Ops:
  7.2 1.0 copy.48
  8.3 1.0 copy.50
  11.0 1.0 copy.46
  12.0 22.7 %all_gather.27 = bf16[128,2048]{1,0:T(8,128)(2,1)S(1)} all-gather(bf16[16,2048]{1,0:T(8,128)(2,1)} %param.19), channel_id=1, replica_groups=mesh['seq'=96,'head'=8] {'head'}, dimensions={0}, use_global_device_ids=true | all-gather | bytes 589824 | tf_op jit(solution)/shard_map/all_gather | solution.py:111
  35.3 1.1 fusion.21
  36.4 103.9 %all-gather.11.cloned.1.call-done = bf16[192,128,128]{2,1,0:T(8,128)(2,1)} async-done(((bf16[2,128,128]{2,1,0:T(8,128)(2,1)}), bf16[192,128,128]{2,1,0:T(8,128)(2,1)}) %all-gather.11.cloned.1.call-update) | async-done | bytes 6291472 | tf_op jit(solution)/shard_map/all_gather | solution.py:16
  140.3 120.7 %all-gather.9.cloned.1.call-done = bf16[192,128,128]{2,1,0:T(8,128)(2,1)} async-done(((bf16[2,128,128]{2,1,0:T(8,128)(2,1)}), bf16[192,128,128]{2,1,0:T(8,128)(2,1)}) %all-gather.9.cloned.1.call-update) | async-done | bytes 6291472 | tf_op jit(solution)/shard_map/all_gather | solution.py:16
  261.1 1.0 while.46
  261.1 0.9 convert_add_fusion.6
  263.0 22.1 %while.48 = (s32[]{:T(128)}, f32[2,2,128,128]{2,3,0,1:T(8,128)S(1)}, f32[2,2,128,128]{2,3,0,1:T(8,128)S(1)}, f32[2,2,128,128]{2,3,0,1:T(8,128)S(1)}, f32[2,2,128...) while((s32[]{:T(128)}, ...), condition=%wide.region_6.7_spmd.clone, body=%wide.region_3.6_spmd.clone.sunk | while | flops 303334912 | bytes 5005465 | solution.py:84
  285.2 1.0 convolution_convert_fusion.1
  290.9 1.2 convolution_convert_fusion
  292.1 195.7 %all-gather.15.cloned.1.call-done = bf16[192,128,128]{2,1,0:T(8,128)(2,1)} async-done(((bf16[2,128,128]{2,1,0:T(8,128)(2,1)}), bf16[192,128,128]{2,1,0:T(8,128)(2,1)}) %all-gather.15.cloned.1.call-update) | async-done | bytes 6291472 | tf_op jit(solution)/shard_map/all_gather | solution.py:38
  487.8 120.6 %all-gather.13.cloned.1.call-done = bf16[192,128,128]{2,1,0:T(8,128)(2,1)} async-done(((bf16[2,128,128]{2,1,0:T(8,128)(2,1)}), bf16[192,128,128]{2,1,0:T(8,128)(2,1)}) %all-gather.13.cloned.1.call-update) | async-done | bytes 6291472 | tf_op jit(solution)/shard_map/all_gather | solution.py:38
  608.4 89.4 %while.47 = (s32[]{:T(128)}, f32[2,128,128]{2,1,0:T(8,128)S(1)}, f32[2,128,128]{2,1,0:T(8,128)S(1)}, s32[]{:T(128)}, bf16[96,2,128,128]{3,2,1,0:T(8,128)(2,1)}, ...) while((s32[]{:T(128)}, f32[2,128,128]{2,1,0:T(8,128)S(1)}, ...), condition=%wide.region_9.10_spmd, body=%wide.region_8.9_spmd.sunk | while | flops 131078 | bytes 655519 | solution.py:55
  608.4 0.9 convert_add_fusion.7
  609.4 0.9 convert_add_fusion.7
  610.3 0.9 convert_add_fusion.7
  611.3 0.9 convert_add_fusion.7
  614.1 0.9 convert_add_fusion.7
  617.0 0.9 convert_add_fusion.7
  617.9 0.9 convert_add_fusion.7
  619.8 0.9 convert_add_fusion.7
  620.8 0.9 convert_add_fusion.7
  623.6 0.9 convert_add_fusion.7
  624.6 0.9 convert_add_fusion.7
  625.6 0.9 convert_add_fusion.7
  628.4 0.9 convert_add_fusion.7
  629.4 0.9 convert_add_fusion.7
  630.3 0.9 convert_add_fusion.7
  631.3 0.9 convert_add_fusion.7
  633.2 0.9 convert_add_fusion.7
  634.1 0.9 convert_add_fusion.7
  636.0 0.9 convert_add_fusion.7
  637.0 0.9 convert_add_fusion.7
  637.9 0.9 convert_add_fusion.7
  638.9 0.9 convert_add_fusion.7
  639.8 0.9 convert_add_fusion.7
  640.8 0.9 convert_add_fusion.7
  641.7 0.9 convert_add_fusion.7
  643.6 0.9 convert_add_fusion.7
  644.6 0.9 convert_add_fusion.7
  646.5 0.9 convert_add_fusion.7
  647.4 0.9 convert_add_fusion.7
  650.3 0.9 convert_add_fusion.7
  653.1 0.9 convert_add_fusion.7
  656.0 0.9 convert_add_fusion.7
  658.8 0.9 convert_add_fusion.7
  661.7 0.9 convert_add_fusion.7
  662.6 0.9 convert_add_fusion.7
  664.5 0.9 convert_add_fusion.7
  665.5 0.9 convert_add_fusion.7
  668.3 0.9 convert_add_fusion.7
  671.2 0.9 convert_add_fusion.7
  674.0 0.9 convert_add_fusion.7
  676.9 0.9 convert_add_fusion.7
  679.7 0.9 convert_add_fusion.7
  680.7 0.9 convert_add_fusion.7
  682.6 0.9 convert_add_fusion.7
  683.5 0.9 convert_add_fusion.7
  686.4 0.9 convert_add_fusion.7
  689.3 0.9 convert_add_fusion.7
  692.1 0.9 convert_add_fusion.7
  695.0 0.9 convert_add_fusion.7
  (210 shorter events, 73.1 us)
Async XLA Ops:
  7.2 27.6 %copy-start = (bf16[256,2048]{1,0:T(8,128)(2,1)S(1)}, bf16[256,2048]{1,0:T(8,128)(2,1)}, u32[]{:S(2)}) copy-start(bf16[256,2048]{1,0:T(8,128)(2,1)} %param.18) | copy-start | bytes 3145732
  7.2 255.8 %copy-start.3 = (s32[1,2]{1,0:T(1,128)S(1)}, s32[1,2]{1,0:T(1,128)}, u32[]{:S(2)}) copy-start(s32[1,2]{1,0:T(1,128)} %param.17) | copy-start | bytes 28
  7.2 255.8 %copy-start.2 = (f32[2]{0:T(128)S(1)}, f32[2]{0:T(128)}, u32[]{:S(2)}) copy-start(f32[2]{0:T(128)} %param.16) | copy-start | bytes 28
  7.2 133.1 %all-gather.11.cloned.1.call-start = ((), (), s32[]{:S(2)}) async-start(), calls=%async_computation.3 | async-start | bytes 6356992 | tf_op jit(solution)/shard_map/all_gather | solution.py:16
  10.1 251.0 %all-gather.9.cloned.1.call-start = ((), (), s32[]{:S(2)}) async-start(), calls=%async_computation.2 | async-start | bytes 6356992 | tf_op jit(solution)/shard_map/all_gather | solution.py:16
  11.0 476.8 %all-gather.15.cloned.1.call-start = ((), (), s32[]{:S(2)}) async-start(), calls=%async_computation.5 | async-start | bytes 6356992 | tf_op jit(solution)/shard_map/all_gather | solution.py:38
  285.1 413.9 %copy-start.1 = (bf16[128,2,128]{2,1,0:T(2,128)(2,1)S(1)}, bf16[128,2,128]{2,1,0:T(2,128)(2,1)}, u32[]{:S(2)}) copy-start(bf16[128,2,128]{2,1,0:T(2,128)(2,1)} %param.15) | copy-start | bytes 196612
  286.3 322.1 %all-gather.13.cloned.1.call-start = ((), (), s32[]{:S(2)}) async-start(), calls=%async_computation.4 | async-start | bytes 6356992 | tf_op jit(solution)/shard_map/all_gather | solution.py:38
  287.4 412.7 %reduce-scatter.2.cloned.1.call-start = ((), (), s32[]{:S(2)}) async-start(), calls=%async_computation.1 | async-start | bytes 589824 | tf_op jit(solution)/shard_map/reduce_scatter | solution.py:129
Sparse Core Ops, SparseCore 0:
  12.3 127.9 all-gather.10
  144.6 116.4 all-gather.8
  286.4 201.3 all-gather.14
  491.9 116.4 all-gather.12
  611.9 33.5 reduce-scatter.1
where the time goes:
time: 711 us; the launch traced here: 707 us
  waiting for transfers between devices  541 us (76%)
  other arithmetic  93.3 us (13%)
  matrix products  26.5 us (4%)
  blocking collectives  22.7 us (3%)
  between operations  14.1 us (2%)
    all_gather x2, waiting for transfers between devices, prefix(): lax.all_gather(a.astype(kind), axis)  316 us
    all_gather x2, waiting for transfers between devices, carried_in(): lax.all_gather(a.astype(kind), axis)  225 us
    add x95, other arithmetic, add_pairs(): return (earlier[0] + later[0], earlier[1] + later[1])  88.1 us
    all_gather x1, blocking collectives, local(): lax.all_gather(d_y, 'head', axis=0, tiled=True)  22.7 us
  transfers between devices with their start and end apart: 5, of which 4 were waited for; matrix products, arithmetic and copies ran while one was open for 14% of the time, Pallas kernels for 0%

commit v1 on v0

v1 whole, which is shorter than its diff:
```python
import functools
import jax
import jax.numpy as jnp
from jax import lax
from jax.experimental import pallas as pl
from jax.experimental.pallas import tpu as pltpu
from jax.sharding import PartitionSpec as P

STEPS_MAX = 12
epsilon = 1e-06
f32 = jnp.float32
bf16 = jnp.bfloat16
N_DIMS = (((1,), (0,)), ((), ()))
T_DIMS = (((1,), (1,)), ((), ()))
L_DIMS = (((0,), (0,)), ((), ()))


def dot(a, b, dims=N_DIMS):
    return lax.dot_general(a, b, dims, preferred_element_type=f32)


def halves(a):
    high = a.astype(bf16)
    return high, (a - high.astype(f32)).astype(bf16)


def wide(a):
    return jnp.concatenate(halves(a), axis=1)


def twice(b):
    return jnp.concatenate([b, b], axis=0)


def causal(rows, transposed=False):
    r = lax.rem(lax.broadcasted_iota(jnp.int32, (rows, 128), 0), 128)
    c = lax.broadcasted_iota(jnp.int32, (rows, 128), 1)
    return (r <= c) if transposed else (r >= c)


def pack(mats, out_ref):
    spans = out_ref.shape[0]
    stack = jnp.concatenate(mats, axis=0).astype(bf16)
    groups = out_ref.shape[1] // 128
    for g in range(groups):
        lo, hi = g * spans, min((g + 1) * spans, 512)
        out_ref[0 : hi - lo, g * 128 : (g + 1) * 128] = stack[lo:hi]
        if hi - lo < spans:
            out_ref[hi - lo : spans, g * 128 : (g + 1) * 128] = jnp.zeros(
                (spans - (hi - lo), 128), bf16
            )


def unpack(ref):
    groups = ref.shape[1] // 128
    stack = jnp.concatenate([ref[:, g * 128 : (g + 1) * 128] for g in range(groups)], axis=0)
    return [stack[i * 128 : (i + 1) * 128] for i in range(4)]


def own_kernel(k_ref, v_ref, out_ref):
    k, v = k_ref[...], v_ref[...]
    mats = []
    for h in range(2):
        mats.append(dot(k[:, h * 128 : (h + 1) * 128], k[:, h * 128 : (h + 1) * 128], L_DIMS))
    for h in range(2):
        mats.append(dot(v[:, h * 128 : (h + 1) * 128], k[:, h * 128 : (h + 1) * 128], L_DIMS))
    pack(mats, out_ref)


def scan_kernel(later, x_ref, out_ref):
    n = x_ref.shape[0]
    r = lax.broadcasted_iota(jnp.int32, (n, n), 0)
    c = lax.broadcasted_iota(jnp.int32, (n, n), 1)
    tri = jnp.where((c > r) if later else (c < r), 1.0, 0.0).astype(bf16)
    out_ref[...] = dot(tri, x_ref[...]).astype(bf16)


def solve_kernel(
    steps_ref,
    reg_ref,
    q_ref,
    k_ref,
    v_ref,
    back_ref,
    pre_ref,
    sol_ref,
    dual_ref,
    mixed_ref,
    grad_q_ref,
    send_ref,
    x_s,
    r_s,
    p_s,
    b_s,
    k_s,
):
    mats = unpack(pre_ref)
    low = causal(128)
    low_two = causal(256)
    for h in range(2):
        lanes = slice(h * 128, (h + 1) * 128)
        k, v, back = k_ref[:, lanes], v_ref[:, lanes], back_ref[:, lanes]
        cov, state = mats[h], mats[2 + h]
        both = jnp.concatenate([cov, k.T], axis=1)
        b_s[h] = twice(both)
        k_s[h] = twice(k)
        firsts = wide(back)
        scores = jnp.where(low, dot(firsts, jnp.concatenate([v, v], axis=1), T_DIMS), 0.0)
        adjoint = dot(firsts, twice(state)) + dot(wide(scores), twice(k))
        right = jnp.concatenate([q_ref[:, lanes].astype(f32), adjoint], axis=0)
        x_s[h] = jnp.zeros_like(right)
        r_s[h] = right
        p_s[h] = right
    rr0 = tuple(jnp.sum(r_s[h] * r_s[h], -1, keepdims=True) for h in range(2))

    def step(i, rrs):
        news = []
        for h in range(2):
            rr = rrs[h]
            p = p_s[h]
            first = dot(wide(p), b_s[h])
            scores = jnp.where(low_two, first[:, 128:], 0.0)
            image = first[:, :128] + dot(wide(scores), k_s[h]) + reg_ref[h] * p
            alpha = rr / (jnp.sum(p * image, -1, keepdims=True) + epsilon)
            kept = jnp.where(i < steps_ref[0, h], alpha, 0.0)
            x_s[h] = x_s[h] + kept * p
            r = r_s[h] - alpha * image
            r_s[h] = r
            new = jnp.sum(r * r, -1, keepdims=True)
            p_s[h] = r + (new / (rr + epsilon)) * p
            news.append(new)
        return tuple(news)

    lax.fori_loop(0, jnp.maximum(steps_ref[0, 0], steps_ref[0, 1]), step, rr0)

    syms, crosses = [], []
    for h in range(2):
        lanes = slice(h * 128, (h + 1) * 128)
        k, v, back = k_ref[:, lanes], v_ref[:, lanes], back_ref[:, lanes]
        state = mats[2 + h]
        sol, dual = x_s[h, :128, :], x_s[h, 128:, :]
        sol_ref[:, lanes] = sol
        dual_ref[:, lanes] = dual
        grad_q_ref[:, lanes] = dual.astype(bf16)
        firsts = wide(sol)
        scores = jnp.where(low, dot(firsts, jnp.concatenate([k, k], axis=1), T_DIMS), 0.0)
        mixed = dot(firsts, jnp.concatenate([state, state], axis=1), T_DIMS) + dot(wide(scores), twice(v))
        mixed_ref[:, lanes] = mixed.astype(bf16)
        sol_high, sol_low = halves(sol)
        dual_high, dual_low = halves(dual)
        back_high, back_low = halves(back)
        outer = dot(
            jnp.concatenate([dual_high, dual_high, dual_low], axis=0),
            jnp.concatenate([sol_high, sol_low, sol_high], axis=0),
            L_DIMS,
        )
        syms.append(outer + outer.T)
        crosses.append(
            dot(
                jnp.concatenate([back_high, back_high, back_low], axis=0),
                jnp.concatenate([sol_high, sol_low, sol_high], axis=0),
                L_DIMS,
            )
        )
    pack(syms + crosses, send_ref)


def inner_kernel(k_ref, v_ref, back_ref, sol_ref, dual_ref, gk_ref, gv_ref):
    up = causal(128, True)
    for h in range(2):
        lanes = slice(h * 128, (h + 1) * 128)
        k, v, back = k_ref[:, lanes], v_ref[:, lanes], back_ref[:, lanes]
        sol, dual = sol_ref[:, lanes], dual_ref[:, lanes]
        kk = jnp.concatenate([k, k], axis=1)
        vv = jnp.concatenate([v, v], axis=1)
        one = wide(jnp.where(up, dot(kk, wide(sol), T_DIMS), 0.0))
        two = wide(jnp.where(up, dot(kk, wide(dual), T_DIMS), 0.0))
        three = wide(jnp.where(up, dot(vv, wide(back), T_DIMS), 0.0))
        sol_b, dual_b, back_b = sol.astype(bf16), dual.astype(bf16), back.astype(bf16)
        gk_ref[:, lanes] = dot(three, twice(sol_b)) - dot(one, twice(dual_b)) - dot(two, twice(sol_b))
        gv_ref[:, lanes] = dot(one, twice(back_b))


def final_kernel(k_ref, v_ref, gk_ref, gv_ref, suf_ref, grad_k_ref, grad_v_ref):
    mats = unpack(suf_ref)
    for h in range(2):
        lanes = slice(h * 128, (h + 1) * 128)
        k, v = k_ref[:, lanes], v_ref[:, lanes]
        sym, cross = mats[h], mats[2 + h]
        grad_k_ref[:, lanes] = (gk_ref[:, lanes] + dot(v, cross) - dot(k, sym)).astype(bf16)
        grad_v_ref[:, lanes] = (gv_ref[:, lanes] + dot(k, cross, T_DIMS)).astype(bf16)


def call(kernel, outs, n_smem=0, n_in=0, scratch=(), flops=0, bytes_accessed=0):
    return pl.pallas_call(
        kernel,
        out_shape=[jax.ShapeDtypeStruct(s, d) for s, d in outs],
        in_specs=[pl.BlockSpec(memory_space=pltpu.SMEM)] * n_smem
        + [pl.BlockSpec(memory_space=pltpu.VMEM)] * n_in,
        out_specs=[pl.BlockSpec(memory_space=pltpu.VMEM)] * len(outs),
        scratch_shapes=list(scratch),
        compiler_params=pltpu.CompilerParams(vmem_limit_bytes=24 * 1024 * 1024),
        cost_estimate=pl.CostEstimate(flops=flops, bytes_accessed=bytes_accessed, transcendentals=0),
    )


def local(queries, keys, values, reg, steps, w_out, d_y):
    size_c, head_count, head_size = queries.shape
    width = head_count * head_size
    spans = lax.axis_size("seq")
    packed = (spans, -(-head_count * 2 * head_size // spans) * head_size)
    tokens = (size_c, width)

    q, k, v = (a.reshape(tokens) for a in (queries, keys, values))

    def exchange(a):
        return lax.all_to_all(a, "seq", 0, 0, tiled=True)

    def scan(a, later):
        return call(functools.partial(scan_kernel, later), [(packed, bf16)], 0, 1)(a)[0]

    (own,) = call(own_kernel, [(packed, bf16)], 0, 2)(k, v)
    dy_rows = lax.all_gather(d_y, "head", axis=0, tiled=True)
    back = lax.dot_general(dy_rows, w_out, T_DIMS, preferred_element_type=f32)
    pre = exchange(scan(exchange(own), False))

    sol, dual, mixed, grad_q, send = call(
        solve_kernel,
        [(tokens, f32), (tokens, f32), (tokens, bf16), (tokens, bf16), (packed, bf16)],
        2,
        5,
        [
            pltpu.VMEM((2, 256, 128), f32),
            pltpu.VMEM((2, 256, 128), f32),
            pltpu.VMEM((2, 256, 128), f32),
            pltpu.VMEM((2, 256, 256), bf16),
            pltpu.VMEM((2, 256, 128), bf16),
        ],
        flops=2 * 10**9,
    )(steps, reg, q, k, v, back, pre)
    out = lax.psum_scatter(
        jnp.dot(mixed, w_out, preferred_element_type=f32).astype(bf16),
        "head",
        scatter_dimension=0,
        tiled=True,
    )
    suf = exchange(scan(exchange(send), True))
    gk, gv = call(inner_kernel, [(tokens, f32), (tokens, f32)], 0, 5, flops=2 * 10**8)(
        k, v, back, sol, dual
    )
    grad_k, grad_v = call(final_kernel, [(tokens, bf16), (tokens, bf16)], 0, 5)(k, v, gk, gv, suf)
    heads = (size_c, head_count, head_size)
    return out, grad_q.reshape(heads), grad_k.reshape(heads), grad_v.reshape(heads)


def solution(mesh):
    placed = (
        P("seq", "head", None),
        P("seq", "head", None),
        P("seq", "head", None),
        P("head"),
        P("seq", "head"),
        P("head", None),
        P(("seq", "head"), None),
    )
    return jax.shard_map(
        local,
        mesh=mesh,
        in_specs=placed,
        out_specs=(
            P(("seq", "head"), None),
            P("seq", "head", None),
            P("seq", "head", None),
            P("seq", "head", None),
        ),
        check_vma=False,
    )
```

time: 711 us -> 152 us (0.21)
  waiting for transfers between devices: 541 us -> 28 us
  other arithmetic: 93.3 us -> 2.74 us
  starting transfers between devices: 0.21 us -> 33.6 us
  blocking collectives: 22.7 us -> 55.8 us
  matrix products: 26.5 us -> 1.59 us
  Pallas kernels: 0 us -> 7.87 us
    all_gather x4 -> x0, waiting for transfers between devices: 541 us -> none  [the longest x2 316 us: prefix(): lax.all_gather(a.astype(kind), axis)]
    add x95 -> x0, other arithmetic: 88.1 us -> none  [add_pairs(): return (earlier[0] + later[0], earlier[1] + later[1])]
    all_to_all x0 -> x3, starting transfers between devices: none -> 33.6 us  [exchange(): return lax.all_to_all(a, 'seq', 0, 0, tiled=True)]
    all_to_all x0 -> x1, blocking collectives: none -> 33.5 us  [exchange(): return lax.all_to_all(a, 'seq', 0, 0, tiled=True)]
    all_to_all x0 -> x3, waiting for transfers between devices: none -> 28 us  [exchange(): return lax.all_to_all(a, 'seq', 0, 0, tiled=True)]
    dot_general x56 -> x2, matrix products: 26.5 us -> 1.59 us  [the longest x1 1.11 us: local(): jnp.dot(mixed, w_out, preferred_element_type=f32).astype(bf16)]
    pallas_call x0 -> x6, Pallas kernels: none -> 7.87 us  [the longest x1 6.48 us: local(): call(solve_kernel, [(tokens, f32), (tokens, f32), (tokens, bf16), (tokens...]
  transfers between devices with their start and end apart: 5 -> 4, of which waited for: 4 -> 2; matrix products, arithmetic and copies ran while one was open for 14% -> 3% of each run, Pallas kernels for 0% -> 1%
where the time goes in v1:
time: 152 us; the launch traced here: 151 us
  blocking collectives  55.8 us (37%)
  starting transfers between devices  33.6 us (22%)
  waiting for transfers between devices  28 us (18%)
  between operations  14.2 us (9%)
  Pallas kernels  7.87 us (5%)
  local copies, waits for them, and re-layouts  6.76 us (4%)
  other arithmetic  2.74 us (2%)
  matrix products  1.59 us (1%)
    all_to_all x3, starting transfers between devices, exchange(): return lax.all_to_all(a, 'seq', 0, 0, tiled=True)  33.6 us
    all_to_all x1, blocking collectives, exchange(): return lax.all_to_all(a, 'seq', 0, 0, tiled=True)  33.5 us
    all_to_all x3, waiting for transfers between devices, exchange(): return lax.all_to_all(a, 'seq', 0, 0, tiled=True)  28 us
    all_gather x1, blocking collectives, local(): dy_rows = lax.all_gather(d_y, 'head', axis=0, tiled=True)  22.3 us
    pallas_call x1, Pallas kernels, local(): call(solve_kernel, [(tokens, f32), (tokens, f32), (tokens, bf16), (tokens...  6.48 us
    unnamed x23, local copies, waits for them, and re-layouts  3.32 us
  transfers between devices with their start and end apart: 4, of which 2 were waited for; matrix products, arithmetic and copies ran while one was open for 3% of the time, Pallas kernels for 1%

profile of v1, /device:TPU:1, one launch (start us, length us, event | category | flops | bytes accessed | tf_op | source)
XLA Modules:
  0.0 150.7 jit_solution(13764741626444655657)
XLA Ops:
  7.2 0.0 copy-start
  7.2 1.0 copy_bitcast_fusion.4
  8.2 0.2 shard_map.102
  8.4 0.5 broadcast
  8.9 0.7 reduce
  9.6 0.7 reshape.40
  10.3 0.0 copy-start.4
  10.3 20.2 %all-to-all-start = ((bf16[96,2,384]{2,1,0:T(2,128)(2,1)}), bf16[96,2,384]{2,1,0:T(2,128)(2,1)S(1)}, u32[]{:S(2)}, u32[]{:S(2)}) async-start(bf16[96,2,384]{2,1,0:T(2,128)(2,1)} %reshape.40), calls=%async_computation | async-start | bytes 294912 | tf_op jit(solution)/shard_map/all_to_all | solution.py:217
  30.4 0.0 copy-done.4
  30.5 14.6 %all-to-all-done = bf16[96,2,384]{2,1,0:T(2,128)(2,1)S(1)} async-done(((bf16[96,2,384]{2,1,0:T(2,128)(2,1)}), bf16[96,2,384]{2,1,0:T(2,128)(2,1)S(1)}, u32[]{:S(2)}, u32[]{:S(2)}) %all-to-all-start) | async-done | bytes 147488 | tf_op jit(solution)/shard_map/all_to_all | solution.py:217
  45.1 0.1 reshape.41
  45.2 0.2 shard_map.103
  45.4 0.7 reduce.1
  46.1 0.7 reshape.42
  46.8 0.0 copy-start.3
  46.8 6.8 %all-to-all-start.1 = ((bf16[96,2,384]{2,1,0:T(2,128)(2,1)}), bf16[96,2,384]{2,1,0:T(2,128)(2,1)S(1)}, u32[]{:S(2)}, u32[]{:S(2)}) async-start(bf16[96,2,384]{2,1,0:T(2,128)(2,1)} %reshape.42), calls=%async_computation.1 | async-start | bytes 294912 | tf_op jit(solution)/shard_map/all_to_all | solution.py:217
  53.5 0.0 reduce-scatter.2.cloned.1.call-start
  53.6 0.0 copy-done.3
  53.6 22.3 %all_gather.3 = bf16[128,2048]{1,0:T(8,128)(2,1)S(1)} all-gather(bf16[16,2048]{1,0:T(8,128)(2,1)S(1)} %copy-done.3), channel_id=1, replica_groups=mesh['seq'=96,'head'=8] {'head'}, dimensions={0}, use_global_device_ids=true | all-gather | bytes 589824 | tf_op jit(solution)/shard_map/all_gather | solution.py:223
  75.9 0.0 copy-done
  75.9 0.5 fusion.back_ref
  76.4 0.0 all-to-all-done.1
  76.4 0.1 reshape.43
  76.6 0.0 copy-start.1
  76.6 0.0 copy-start.2
  76.6 0.6 copy-done.1
  77.2 0.0 copy-done.2
  77.2 6.5 %shard_map.104 = (f32[128,256]{1,0:T(8,128)S(1)}, f32[128,256]{1,0:T(8,128)S(1)}, bf16[128,256]{1,0:T(8,128)(2,1)S(1)}, bf16[128,256]{1,0:T(8,128)(2,1)S(1)}, bf16[96,768]{1,0:T(8,128)(2,1)S(1)}) custom-call(s32[1,2]{1,0:T(1,128)S(1)} %copy-done.1, f32[2]{0:T(128)S(1)} %copy-done.2, bf16[128,256]{1,0:T(8,128)(2,1)S(1)} %bitcast.38, ...), custom_call_target="tpu_custom_call" | custom-call | flops 2000000000 | tf_op jit(solution)/shard_map/pallas_call | solution.py:227
  83.7 1.1 convolution_convert_fusion
  84.8 0.0 reduce-scatter.2.cloned.1.call-update
  84.8 0.7 reduce.2
  85.6 33.5 %all_to_all.44 = bf16[96,2,384]{2,1,0:T(2,128)(2,1)S(1)} all-to-all(bf16[96,2,384]{2,1,0:T(2,128)(2,1)S(1)} %reshape.44), channel_id=1, replica_groups=mesh['seq'=96,'head'=8] {'seq'}, dimensions={0} | all-to-all | bytes 294912 | tf_op jit(solution)/shard_map/all_to_all | solution.py:217
  119.0 0.1 reshape.45
  119.2 0.2 shard_map.106
  119.4 0.7 reduce.3
  120.1 0.7 reshape.46
  120.7 6.7 %all-to-all-start.3 = ((bf16[96,2,384]{2,1,0:T(2,128)(2,1)}), bf16[96,2,384]{2,1,0:T(2,128)(2,1)S(1)}, u32[]{:S(2)}, u32[]{:S(2)}) async-start(bf16[96,2,384]{2,1,0:T(2,128)(2,1)} %reshape.46), calls=%async_computation.4 | async-start | bytes 294912 | tf_op jit(solution)/shard_map/all_to_all | solution.py:217
  127.4 0.7 reshape.37
  128.1 0.6 shard_map.105
  128.7 13.4 %all-to-all-done.3 = bf16[96,2,384]{2,1,0:T(2,128)(2,1)S(1)} async-done(((bf16[96,2,384]{2,1,0:T(2,128)(2,1)}), bf16[96,2,384]{2,1,0:T(2,128)(2,1)S(1)}, u32[]{:S(2)}, u32[]{:S(2)}) %all-to-all-start.3) | async-done | bytes 147488 | tf_op jit(solution)/shard_map/all_to_all | solution.py:217
  142.1 0.1 reshape.47
  142.3 0.2 shard_map.107
  142.5 0.7 reshape.38
  143.2 0.6 reshape.39
  143.8 0.0 reduce-scatter.2.cloned.1.call-done
  (6 shorter events, 0.1 us)
Async XLA Ops:
  7.2 68.7 %copy-start = (bf16[256,2048]{1,0:T(8,128)(2,1)S(1)}, bf16[256,2048]{1,0:T(8,128)(2,1)}, u32[]{:S(2)}) copy-start(bf16[256,2048]{1,0:T(8,128)(2,1)} %param.12) | copy-start | bytes 3145732
  10.3 20.2 %copy-start.4 = (bf16[128,2,128]{2,1,0:T(2,128)(2,1)S(1)}, bf16[128,2,128]{2,1,0:T(2,128)(2,1)}, u32[]{:S(2)}) copy-start(bf16[128,2,128]{2,1,0:T(2,128)(2,1)} %param.7) | copy-start | bytes 196612
  10.3 34.8 %all-to-all-start = ((bf16[96,2,384]{2,1,0:T(2,128)(2,1)}), bf16[96,2,384]{2,1,0:T(2,128)(2,1)S(1)}, u32[]{:S(2)}, u32[]{:S(2)}) async-start(bf16[96,2,384]{2,1,0:T(2,128)(2,1)} %reshape.40), calls=%async_computation | async-start | bytes 294912 | tf_op jit(solution)/shard_map/all_to_all | solution.py:217
  46.8 6.8 %copy-start.3 = (bf16[16,2048]{1,0:T(8,128)(2,1)S(1)}, bf16[16,2048]{1,0:T(8,128)(2,1)}, u32[]{:S(2)}) copy-start(bf16[16,2048]{1,0:T(8,128)(2,1)} %param.13) | copy-start | bytes 196612
  46.8 29.6 %all-to-all-start.1 = ((bf16[96,2,384]{2,1,0:T(2,128)(2,1)}), bf16[96,2,384]{2,1,0:T(2,128)(2,1)S(1)}, u32[]{:S(2)}, u32[]{:S(2)}) async-start(bf16[96,2,384]{2,1,0:T(2,128)(2,1)} %reshape.42), calls=%async_computation.1 | async-start | bytes 294912 | tf_op jit(solution)/shard_map/all_to_all | solution.py:217
  53.5 90.3 %reduce-scatter.2.cloned.1.call-start = ((), (), s32[]{:S(2)}) async-start(), calls=%async_computation.5 | async-start | bytes 589824 | tf_op jit(solution)/shard_map/reduce_scatter | solution.py:241
  76.6 0.7 copy-start.1
  76.6 0.7 copy-start.2
  120.7 21.4 %all-to-all-start.3 = ((bf16[96,2,384]{2,1,0:T(2,128)(2,1)}), bf16[96,2,384]{2,1,0:T(2,128)(2,1)S(1)}, u32[]{:S(2)}, u32[]{:S(2)}) async-start(bf16[96,2,384]{2,1,0:T(2,128)(2,1)} %reshape.46), calls=%async_computation.4 | async-start | bytes 294912 | tf_op jit(solution)/shard_map/all_to_all | solution.py:217
Sparse Core Ops, SparseCore 0:
  85.0 43.3 reduce-scatter.1

commit v2 on v1

--- a/solution.py
+++ b/solution.py
@@ -38,40 +38,46 @@
     return (r <= c) if transposed else (r >= c)
 
 
+ROWS = 6
+STACK = 512
+
+
+def heads_apart(both):
+    head = lax.rem(lax.broadcasted_iota(jnp.int32, (256, 1), 0), 2)
+    first = jnp.where(head == 0, 1.0, 0.0).astype(bf16)
+    return jnp.concatenate([both * first, both * (1 - first)], axis=1)
+
+
 def pack(mats, out_ref):
-    spans = out_ref.shape[0]
-    stack = jnp.concatenate(mats, axis=0).astype(bf16)
-    groups = out_ref.shape[1] // 128
-    for g in range(groups):
-        lo, hi = g * spans, min((g + 1) * spans, 512)
-        out_ref[0 : hi - lo, g * 128 : (g + 1) * 128] = stack[lo:hi]
-        if hi - lo < spans:
-            out_ref[hi - lo : spans, g * 128 : (g + 1) * 128] = jnp.zeros(
-                (spans - (hi - lo), 128), bf16
-            )
+    for i, mat in enumerate(mats):
+        out_ref[i * 128 : (i + 1) * 128, :] = mat.astype(bf16)
+    rest = out_ref.shape[0] - STACK
+    out_ref[STACK:, :] = jnp.zeros((rest, 128), bf16)
 
 
 def unpack(ref):
-    groups = ref.shape[1] // 128
-    stack = jnp.concatenate([ref[:, g * 128 : (g + 1) * 128] for g in range(groups)], axis=0)
-    return [stack[i * 128 : (i + 1) * 128] for i in range(4)]
+    return [ref[i * 128 : (i + 1) * 128, :] for i in range(4)]
 
 
 def own_kernel(k_ref, v_ref, out_ref):
-    k, v = k_ref[...], v_ref[...]
-    mats = []
-    for h in range(2):
-        mats.append(dot(k[:, h * 128 : (h + 1) * 128], k[:, h * 128 : (h + 1) * 128], L_DIMS))
-    for h in range(2):
-        mats.append(dot(v[:, h * 128 : (h + 1) * 128], k[:, h * 128 : (h + 1) * 128], L_DIMS))
-    pack(mats, out_ref)
+    k = k_ref[...]
+    sums = dot(heads_apart(k), k, L_DIMS)
+    states = dot(heads_apart(v_ref[...]), k, L_DIMS)
+    pack([sums[:128], sums[128:], states[:128], states[128:]], out_ref)
 
 
 def scan_kernel(later, x_ref, out_ref):
     n = x_ref.shape[0]
-    r = lax.broadcasted_iota(jnp.int32, (n, n), 0)
-    c = lax.broadcasted_iota(jnp.int32, (n, n), 1)
-    tri = jnp.where((c > r) if later else (c < r), 1.0, 0.0).astype(bf16)
+
+    def place(shape, dim):
+        i = lax.broadcasted_iota(jnp.int32, shape, dim)
+        span = lax.shift_right_logical(i * 10923, 16)
+        return span, i - ROWS * span
+
+    r_span, r_row = place((n, 1), 0)
+    c_span, c_row = place((1, n), 1)
+    reach = (c_span > r_span) if later else (c_span < r_span)
+    tri = jnp.where(reach & (r_row == c_row), 1.0, 0.0).astype(bf16)
     out_ref[...] = dot(tri, x_ref[...]).astype(bf16)
 
 
@@ -182,13 +188,13 @@
 
 
 def final_kernel(k_ref, v_ref, gk_ref, gv_ref, suf_ref, grad_k_ref, grad_v_ref):
-    mats = unpack(suf_ref)
-    for h in range(2):
-        lanes = slice(h * 128, (h + 1) * 128)
-        k, v = k_ref[:, lanes], v_ref[:, lanes]
-        sym, cross = mats[h], mats[2 + h]
-        grad_k_ref[:, lanes] = (gk_ref[:, lanes] + dot(v, cross) - dot(k, sym)).astype(bf16)
-        grad_v_ref[:, lanes] = (gv_ref[:, lanes] + dot(k, cross, T_DIMS)).astype(bf16)
+    sym0, sym1, cross0, cross1 = unpack(suf_ref)
+    k, v = heads_apart(k_ref[...]), heads_apart(v_ref[...])
+    cross = jnp.concatenate([cross0, cross1], axis=0)
+    sym = jnp.concatenate([sym0, sym1], axis=0)
+    cross_lanes = jnp.concatenate([cross0, cross1], axis=1)
+    grad_k_ref[...] = (gk_ref[...] + dot(v, cross) - dot(k, sym)).astype(bf16)
+    grad_v_ref[...] = (gv_ref[...] + dot(k, cross_lanes, T_DIMS)).astype(bf16)
 
 
 def call(kernel, outs, n_smem=0, n_in=0, scratch=(), flops=0, bytes_accessed=0):
@@ -208,20 +214,27 @@
     size_c, head_count, head_size = queries.shape
     width = head_count * head_size
     spans = lax.axis_size("seq")
-    packed = (spans, -(-head_count * 2 * head_size // spans) * head_size)
+    packed = (spans * ROWS, head_size)
     tokens = (size_c, width)
-
-    q, k, v = (a.reshape(tokens) for a in (queries, keys, values))
+    pairs = (size_c * head_count, head_size)
+    heads = (size_c, head_count, head_size)
 
     def exchange(a):
-        return lax.all_to_all(a, "seq", 0, 0, tiled=True)
+        parts = a.reshape(spans, ROWS // 2, 2, head_size).transpose(0, 2, 1, 3)
+        moved = lax.all_to_all(parts.reshape(spans, 2, -1), "seq", 0, 0)
+        parts = moved.reshape(spans, 2, ROWS // 2, head_size).transpose(0, 2, 1, 3)
+        return parts.reshape(packed)
 
     def scan(a, later):
         return call(functools.partial(scan_kernel, later), [(packed, bf16)], 0, 1)(a)[0]
 
-    (own,) = call(own_kernel, [(packed, bf16)], 0, 2)(k, v)
-    dy_rows = lax.all_gather(d_y, "head", axis=0, tiled=True)
+    k_pairs, v_pairs = keys.reshape(pairs), values.reshape(pairs)
+    (own,) = call(own_kernel, [(packed, bf16)], 0, 2)(k_pairs, v_pairs)
+    rows = d_y.shape[0]
+    dy_rows = lax.all_gather(jnp.concatenate([d_y, d_y], axis=0), "head", axis=0, tiled=True)
     back = lax.dot_general(dy_rows, w_out, T_DIMS, preferred_element_type=f32)
+    back = back.reshape(-1, 2 * rows, width)[:, :rows].reshape(tokens)
+    q, k, v = (a.reshape(tokens) for a in (queries, keys, values))
     pre = exchange(scan(exchange(own), False))
 
     sol, dual, mixed, grad_q, send = call(
@@ -248,8 +261,9 @@
     gk, gv = call(inner_kernel, [(tokens, f32), (tokens, f32)], 0, 5, flops=2 * 10**8)(
         k, v, back, sol, dual
     )
-    grad_k, grad_v = call(final_kernel, [(tokens, bf16), (tokens, bf16)], 0, 5)(k, v, gk, gv, suf)
-    heads = (size_c, head_count, head_size)
+    grad_k, grad_v = call(final_kernel, [(pairs, bf16), (pairs, bf16)], 0, 5)(
+        k_pairs, v_pairs, gk.reshape(heads).reshape(pairs), gv.reshape(heads).reshape(pairs), suf
+    )
     return out, grad_q.reshape(heads), grad_k.reshape(heads), grad_v.reshape(heads)
 
 

time: 152 us -> 134 us (0.88)
  blocking collectives: 55.8 us -> 28.7 us
  waiting for transfers between devices: 28 us -> 41 us
  local copies, waits for them, and re-layouts: 6.76 us -> 2.24 us
    all_gather x1 -> x0, blocking collectives: 22.3 us -> none  [local(): dy_rows = lax.all_gather(d_y, 'head', axis=0, tiled=True)]
    all_to_all x3, waiting for transfers between devices: 28 us -> 36.5 us  [exchange(): moved = lax.all_to_all(parts.reshape(spans, 2, -1), 'seq', 0, 0)]
    all_to_all x1, blocking collectives: 33.5 us -> 28.7 us  [exchange(): moved = lax.all_to_all(parts.reshape(spans, 2, -1), 'seq', 0, 0)]
    all_gather x0 -> x1, waiting for transfers between devices: none -> 4.39 us  [local(): lax.all_gather(jnp.concatenate([d_y, d_y], axis=0), 'head', axis=0, tiled...]
    pallas_call x1, Pallas kernels: 6.48 us -> 2.97 us  [local(): call(solve_kernel, [(tokens, f32), (tokens, f32), (tokens, bf16), (tokens...]
    all_to_all x4 -> x0, other arithmetic: 2.74 us -> none  [exchange(): return lax.all_to_all(a, 'seq', 0, 0, tiled=True)]
    unnamed x23 -> x13, local copies, waits for them, and re-layouts: 3.32 us -> 1.54 us
    pallas_call x2, Pallas kernels: 0.34 us -> 2.08 us  [scan(): call(functools.partial(scan_kernel, later), [(packed, bf16)], 0, 1)(a)[0]]
  transfers between devices with their start and end apart: 4 -> 5, of which waited for: 2 -> 4; matrix products, arithmetic and copies ran while one was open for 3% -> 2% of each run, Pallas kernels for 1% -> 3%
where the time goes in v2:
time: 134 us; the launch traced here: 132 us
  waiting for transfers between devices  41 us (31%)
  starting transfers between devices  33.6 us (25%)
  blocking collectives  28.7 us (21%)
  between operations  14.1 us (11%)
  Pallas kernels  7.55 us (6%)
  matrix products  2.8 us (2%)
  local copies, waits for them, and re-layouts  2.24 us (2%)
  other arithmetic  1.6 us (1%)
    all_to_all x3, waiting for transfers between devices, exchange(): moved = lax.all_to_all(parts.reshape(spans, 2, -1), 'seq', 0, 0)  36.5 us
    all_to_all x3, starting transfers between devices, exchange(): moved = lax.all_to_all(parts.reshape(spans, 2, -1), 'seq', 0, 0)  33.5 us
    all_to_all x1, blocking collectives, exchange(): moved = lax.all_to_all(parts.reshape(spans, 2, -1), 'seq', 0, 0)  28.7 us
    all_gather x1, waiting for transfers between devices, local(): lax.all_gather(jnp.concatenate([d_y, d_y], axis=0), 'head', axis=0, tiled...  4.39 us
    pallas_call x1, Pallas kernels, local(): call(solve_kernel, [(tokens, f32), (tokens, f32), (tokens, bf16), (tokens...  2.97 us
  transfers between devices with their start and end apart: 5, of which 4 were waited for; matrix products, arithmetic and copies ran while one was open for 2% of the time, Pallas kernels for 3%

profile of v2, /device:TPU:1, one launch (start us, length us, event | category | flops | bytes accessed | tf_op | source)
XLA Modules:
  0.0 131.5 jit_solution(10399204660404556319)
XLA Ops:
  7.2 0.0 copy-start
  7.2 0.0 all-gather.2.cloned.1.call-start
  7.2 1.6 %pad_maximum_fusion = bf16[32,2048]{1,0:T(8,128)(2,1)} fusion(bf16[16,2048]{1,0:T(8,128)(2,1)} %param.13), kind=kLoop, calls=%fused_computation.1 | loop fusion | flops 262144 | bytes 196608 | tf_op jit(solution)/shard_map/concatenate | solution.py:234
  8.8 0.0 copy-start.1
  8.8 0.0 copy-start.2
  8.8 0.0 all-gather.2.cloned.1.call-update
  8.9 0.8 copy-done.1
  9.7 0.0 copy-done.2
  9.7 1.0 shard_map.102
  10.7 0.0 copy-start.5
  10.7 20.2 %all-to-all-start = ((bf16[96,2,384]{2,1,0:T(2,128)(2,1)}), bf16[96,2,384]{2,1,0:T(2,128)(2,1)S(1)}, u32[]{:S(2)}, u32[]{:S(2)}) async-start(bf16[96,2,384]{2,1,0:T(2,128)(2,1)} %bitcast.6), calls=%async_computation | async-start | bytes 294912 | tf_op jit(solution)/shard_map/all_to_all | solution.py:224
  30.8 0.0 copy-done.5
  30.9 14.6 %all-to-all-done = bf16[96,2,384]{2,1,0:T(2,128)(2,1)S(1)} async-done(((bf16[96,2,384]{2,1,0:T(2,128)(2,1)}), bf16[96,2,384]{2,1,0:T(2,128)(2,1)S(1)}, u32[]{:S(2)}, u32[]{:S(2)}) %all-to-all-start) | async-done | bytes 147488 | tf_op jit(solution)/shard_map/all_to_all | solution.py:224
  45.4 1.1 shard_map.103
  46.5 6.7 %all-to-all-start.1 = ((bf16[96,2,384]{2,1,0:T(2,128)(2,1)}), bf16[96,2,384]{2,1,0:T(2,128)(2,1)S(1)}, u32[]{:S(2)}, u32[]{:S(2)}) async-start(bf16[96,2,384]{2,1,0:T(2,128)(2,1)} %bitcast.12), calls=%async_computation.1 | async-start | bytes 294912 | tf_op jit(solution)/shard_map/all_to_all | solution.py:224
  53.2 0.0 reduce-scatter.2.cloned.1.call-start
  53.2 4.4 %all-gather.2.cloned.1.call-done = bf16[256,2048]{1,0:T(8,128)(2,1)} async-done(((bf16[32,2048]{1,0:T(8,128)(2,1)}), bf16[256,2048]{1,0:T(8,128)(2,1)}) %all-gather.2.cloned.1.call-update) | async-done | bytes 1048592 | tf_op jit(solution)/shard_map/all_gather | solution.py:234
  57.6 0.0 copy-done
  57.6 1.7 %fusion = f32[256,256]{1,0:T(8,128)S(1)} fusion(bf16[256,2048]{1,0:T(8,128)(2,1)} %all-gather.2.cloned.1.call-done, bf16[256,2048]{1,0:T(8,128)(2,1)S(1)} %copy-done), kind=kOutput, calls=%fused_computation.5 | convolution fusion | flops 268435456 | bytes 2359296 | tf_op jit(solution)/shard_map/dot_general | solution.py:235
  59.4 8.5 %all-to-all-done.1 = bf16[96,2,384]{2,1,0:T(2,128)(2,1)S(1)} async-done(((bf16[96,2,384]{2,1,0:T(2,128)(2,1)}), bf16[96,2,384]{2,1,0:T(2,128)(2,1)S(1)}, u32[]{:S(2)}, u32[]{:S(2)}) %all-to-all-start.1) | async-done | bytes 147488 | tf_op jit(solution)/shard_map/all_to_all | solution.py:224
  67.9 0.0 copy-start.3
  67.9 0.0 copy-start.4
  67.9 0.7 copy-done.3
  68.6 0.0 copy-done.4
  68.6 3.0 %shard_map.104 = (f32[128,256]{1,0:T(8,128)S(1)}, f32[128,256]{1,0:T(8,128)S(1)}, bf16[128,256]{1,0:T(8,128)(2,1)S(1)}, bf16[128,256]{1,0:T(8,128)(2,1)S(1)}, bf16[576,128]{1,0:T(8,128)(2,1)S(1)}) custom-call(s32[1,2]{1,0:T(1,128)S(1)} %copy-done.3, f32[2]{0:T(128)S(1)} %copy-done.4, bf16[128,256]{1,0:T(8,128)(2,1)S(1)} %bitcast.73, ...), custom_call_target="tpu_custom_call" | custom-call | flops 2000000000 | tf_op jit(solution)/shard_map/pallas_call | solution.py:240
  71.5 1.1 convolution_convert_fusion
  72.7 0.0 reduce-scatter.2.cloned.1.call-update
  72.7 28.7 %all_to_all.20 = bf16[96,2,384]{2,1,0:T(2,128)(2,1)S(1)} all-to-all(bf16[96,2,384]{2,1,0:T(2,128)(2,1)S(1)} %bitcast.70), channel_id=1, replica_groups=mesh['seq'=96,'head'=8] {'seq'}, dimensions={0} | all-to-all | bytes 294912 | tf_op jit(solution)/shard_map/all_to_all | solution.py:224
  101.4 1.0 shard_map.106
  102.4 6.7 %all-to-all-start.3 = ((bf16[96,2,384]{2,1,0:T(2,128)(2,1)}), bf16[96,2,384]{2,1,0:T(2,128)(2,1)S(1)}, u32[]{:S(2)}, u32[]{:S(2)}) async-start(bf16[96,2,384]{2,1,0:T(2,128)(2,1)} %bitcast.24), calls=%async_computation.4 | async-start | bytes 294912 | tf_op jit(solution)/shard_map/all_to_all | solution.py:224
  109.1 0.6 shard_map.105
  109.7 0.7 reshape.101
  110.4 13.4 %all-to-all-done.3 = bf16[96,2,384]{2,1,0:T(2,128)(2,1)S(1)} async-done(((bf16[96,2,384]{2,1,0:T(2,128)(2,1)}), bf16[96,2,384]{2,1,0:T(2,128)(2,1)S(1)}, u32[]{:S(2)}, u32[]{:S(2)}) %all-to-all-start.3) | async-done | bytes 147488 | tf_op jit(solution)/shard_map/all_to_all | solution.py:224
  123.8 0.9 shard_map.107
  124.7 0.0 reduce-scatter.2.cloned.1.call-done
  (5 shorter events, 0.1 us)
Async XLA Ops:
  7.2 50.5 %copy-start = (bf16[256,2048]{1,0:T(8,128)(2,1)S(1)}, bf16[256,2048]{1,0:T(8,128)(2,1)}, u32[]{:S(2)}) copy-start(bf16[256,2048]{1,0:T(8,128)(2,1)} %param.12) | copy-start | bytes 3145732
  7.2 50.5 %all-gather.2.cloned.1.call-start = ((), (), s32[]{:S(2)}) async-start(), calls=%async_computation.5 | async-start | bytes 1179648 | tf_op jit(solution)/shard_map/all_gather | solution.py:234
  8.8 0.8 copy-start.1
  8.8 0.9 copy-start.2
  10.7 20.2 %copy-start.5 = (bf16[128,2,128]{2,1,0:T(2,128)(2,1)S(1)}, bf16[128,2,128]{2,1,0:T(2,128)(2,1)}, u32[]{:S(2)}) copy-start(bf16[128,2,128]{2,1,0:T(2,128)(2,1)} %param.7) | copy-start | bytes 196612
  10.7 34.8 %all-to-all-start = ((bf16[96,2,384]{2,1,0:T(2,128)(2,1)}), bf16[96,2,384]{2,1,0:T(2,128)(2,1)S(1)}, u32[]{:S(2)}, u32[]{:S(2)}) async-start(bf16[96,2,384]{2,1,0:T(2,128)(2,1)} %bitcast.6), calls=%async_computation | async-start | bytes 294912 | tf_op jit(solution)/shard_map/all_to_all | solution.py:224
  46.5 21.4 %all-to-all-start.1 = ((bf16[96,2,384]{2,1,0:T(2,128)(2,1)}), bf16[96,2,384]{2,1,0:T(2,128)(2,1)S(1)}, u32[]{:S(2)}, u32[]{:S(2)}) async-start(bf16[96,2,384]{2,1,0:T(2,128)(2,1)} %bitcast.12), calls=%async_computation.1 | async-start | bytes 294912 | tf_op jit(solution)/shard_map/all_to_all | solution.py:224
  53.2 71.5 %reduce-scatter.2.cloned.1.call-start = ((), (), s32[]{:S(2)}) async-start(), calls=%async_computation.6 | async-start | bytes 589824 | tf_op jit(solution)/shard_map/reduce_scatter | solution.py:254
  67.9 0.7 copy-start.3
  67.9 0.7 copy-start.4
  102.4 21.4 %all-to-all-start.3 = ((bf16[96,2,384]{2,1,0:T(2,128)(2,1)}), bf16[96,2,384]{2,1,0:T(2,128)(2,1)S(1)}, u32[]{:S(2)}, u32[]{:S(2)}) async-start(bf16[96,2,384]{2,1,0:T(2,128)(2,1)} %bitcast.24), calls=%async_computation.4 | async-start | bytes 294912 | tf_op jit(solution)/shard_map/all_to_all | solution.py:224
Sparse Core Ops, SparseCore 0:
  10.4 47.2 all-gather.1
  72.8 39.4 reduce-scatter.1

commit v3 on v2

--- a/solution.py
+++ b/solution.py
@@ -4,9 +4,11 @@
 from jax import lax
 from jax.experimental import pallas as pl
 from jax.experimental.pallas import tpu as pltpu
+from jax.sharding import Mesh
 from jax.sharding import PartitionSpec as P
 
 STEPS_MAX = 12
+SEQ = ("chip", "core")
 epsilon = 1e-06
 f32 = jnp.float32
 bf16 = jnp.bfloat16
@@ -59,31 +61,48 @@
     return [ref[i * 128 : (i + 1) * 128, :] for i in range(4)]
 
 
+def heads_apart_turned(both):
+    turned = both.T
+    head = lax.rem(lax.broadcasted_iota(jnp.int32, (1, 256), 1), 2)
+    first = jnp.where(head == 0, 1.0, 0.0).astype(bf16)
+    return jnp.concatenate([turned * first, turned * (1 - first)], axis=0)
+
+
 def own_kernel(k_ref, v_ref, out_ref):
     k = k_ref[...]
-    sums = dot(heads_apart(k), k, L_DIMS)
-    states = dot(heads_apart(v_ref[...]), k, L_DIMS)
+    sums = dot(heads_apart_turned(k), k)
+    states = dot(heads_apart_turned(v_ref[...]), k)
     pack([sums[:128], sums[128:], states[:128], states[128:]], out_ref)
 
 
 def scan_kernel(later, x_ref, out_ref):
-    n = x_ref.shape[0]
+    size = 16 * ROWS
+    blocks = x_ref.shape[0] // size
 
     def place(shape, dim):
         i = lax.broadcasted_iota(jnp.int32, shape, dim)
         span = lax.shift_right_logical(i * 10923, 16)
         return span, i - ROWS * span
 
-    r_span, r_row = place((n, 1), 0)
-    c_span, c_row = place((1, n), 1)
+    r_span, r_row = place((size, 1), 0)
+    c_span, c_row = place((1, size), 1)
+    same = r_row == c_row
     reach = (c_span > r_span) if later else (c_span < r_span)
-    tri = jnp.where(reach & (r_row == c_row), 1.0, 0.0).astype(bf16)
-    out_ref[...] = dot(tri, x_ref[...]).astype(bf16)
+    tri = jnp.where(reach & same, 1.0, 0.0)
+    every = jnp.where(same, 1.0, 0.0)
+    side = jnp.concatenate([x_ref[g * size : (g + 1) * size, :] for g in range(blocks)], axis=1)
+    sums = dot(jnp.concatenate([tri, every], axis=0).astype(bf16), side)
+    carry = None
+    for g in reversed(range(blocks)) if later else range(blocks):
+        lanes = slice(g * 128, (g + 1) * 128)
+        inside = sums[:size, lanes]
+        out_ref[g * size : (g + 1) * size, :] = (inside if carry is None else inside + carry).astype(bf16)
+        total = sums[size:, lanes]
+        carry = total if carry is None else carry + total
 
 
 def solve_kernel(
-    steps_ref,
-    reg_ref,
+    cfg_ref,
     q_ref,
     k_ref,
     v_ref,
@@ -103,6 +122,9 @@
     mats = unpack(pre_ref)
     low = causal(128)
     low_two = causal(256)
+    ridges = [jnp.broadcast_to(cfg_ref[:, h : h + 1], (1, 128)) for h in range(2)]
+    counts = [cfg_ref[:, 2 + h : 3 + h] for h in range(2)]
+    rrs = []
     for h in range(2):
         lanes = slice(h * 128, (h + 1) * 128)
         k, v, back = k_ref[:, lanes], v_ref[:, lanes], back_ref[:, lanes]
@@ -117,27 +139,25 @@
         x_s[h] = jnp.zeros_like(right)
         r_s[h] = right
         p_s[h] = right
-    rr0 = tuple(jnp.sum(r_s[h] * r_s[h], -1, keepdims=True) for h in range(2))
-
-    def step(i, rrs):
-        news = []
+        rrs.append(jnp.sum(right * right, -1, keepdims=True))
+
+    for i in range(STEPS_MAX):
+        ps = [p_s[h] for h in range(2)]
+        firsts = [dot(wide(ps[h]), b_s[h]) for h in range(2)]
+        scores = [jnp.where(low_two, firsts[h][:, 128:], 0.0) for h in range(2)]
+        seconds = [dot(wide(scores[h]), k_s[h]) for h in range(2)]
+        images = [firsts[h][:, :128] + seconds[h] + ridges[h] * ps[h] for h in range(2)]
+        alphas = [rrs[h] / (jnp.sum(ps[h] * images[h], -1, keepdims=True) + epsilon) for h in range(2)]
         for h in range(2):
-            rr = rrs[h]
-            p = p_s[h]
-            first = dot(wide(p), b_s[h])
-            scores = jnp.where(low_two, first[:, 128:], 0.0)
-            image = first[:, :128] + dot(wide(scores), k_s[h]) + reg_ref[h] * p
-            alpha = rr / (jnp.sum(p * image, -1, keepdims=True) + epsilon)
-            kept = jnp.where(i < steps_ref[0, h], alpha, 0.0)
-            x_s[h] = x_s[h] + kept * p
-            r = r_s[h] - alpha * image
+            kept = jnp.where(i < counts[h], alphas[h], 0.0)
+            x_s[h] = x_s[h] + kept * ps[h]
+            if i == STEPS_MAX - 1:
+                continue
+            r = r_s[h] - alphas[h] * images[h]
             r_s[h] = r
             new = jnp.sum(r * r, -1, keepdims=True)
-            p_s[h] = r + (new / (rr + epsilon)) * p
-            news.append(new)
-        return tuple(news)
-
-    lax.fori_loop(0, jnp.maximum(steps_ref[0, 0], steps_ref[0, 1]), step, rr0)
+            p_s[h] = r + (new / (rrs[h] + epsilon)) * ps[h]
+            rrs[h] = new
 
     syms, crosses = [], []
     for h in range(2):
@@ -197,7 +217,7 @@
     grad_v_ref[...] = (gv_ref[...] + dot(k, cross_lanes, T_DIMS)).astype(bf16)
 
 
-def call(kernel, outs, n_smem=0, n_in=0, scratch=(), flops=0, bytes_accessed=0):
+def call(kernel, outs, n_smem=0, n_in=0, scratch=(), flops=0, bytes_accessed=0, vmem=24):
     return pl.pallas_call(
         kernel,
         out_shape=[jax.ShapeDtypeStruct(s, d) for s, d in outs],
@@ -205,7 +225,7 @@
         + [pl.BlockSpec(memory_space=pltpu.VMEM)] * n_in,
         out_specs=[pl.BlockSpec(memory_space=pltpu.VMEM)] * len(outs),
         scratch_shapes=list(scratch),
-        compiler_params=pltpu.CompilerParams(vmem_limit_bytes=24 * 1024 * 1024),
+        compiler_params=pltpu.CompilerParams(vmem_limit_bytes=vmem * 1024 * 1024),
         cost_estimate=pl.CostEstimate(flops=flops, bytes_accessed=bytes_accessed, transcendentals=0),
     )
 
@@ -213,7 +233,7 @@
 def local(queries, keys, values, reg, steps, w_out, d_y):
     size_c, head_count, head_size = queries.shape
     width = head_count * head_size
-    spans = lax.axis_size("seq")
+    spans = lax.axis_size(SEQ)
     packed = (spans * ROWS, head_size)
     tokens = (size_c, width)
     pairs = (size_c * head_count, head_size)
@@ -221,7 +241,7 @@
 
     def exchange(a):
         parts = a.reshape(spans, ROWS // 2, 2, head_size).transpose(0, 2, 1, 3)
-        moved = lax.all_to_all(parts.reshape(spans, 2, -1), "seq", 0, 0)
+        moved = lax.all_to_all(parts.reshape(spans, 2, -1), SEQ, 0, 0)
         parts = moved.reshape(spans, 2, ROWS // 2, head_size).transpose(0, 2, 1, 3)
         return parts.reshape(packed)
 
@@ -229,19 +249,19 @@
         return call(functools.partial(scan_kernel, later), [(packed, bf16)], 0, 1)(a)[0]
 
     k_pairs, v_pairs = keys.reshape(pairs), values.reshape(pairs)
-    (own,) = call(own_kernel, [(packed, bf16)], 0, 2)(k_pairs, v_pairs)
-    rows = d_y.shape[0]
-    dy_rows = lax.all_gather(jnp.concatenate([d_y, d_y], axis=0), "head", axis=0, tiled=True)
+    (own,) = call(own_kernel, [(packed, bf16)], 0, 2, vmem=56)(k_pairs, v_pairs)
+    dy_rows = lax.all_gather(d_y, ("core", "head"), axis=0, tiled=True)
+    dy_rows = lax.dynamic_slice_in_dim(dy_rows, lax.axis_index("core") * size_c, size_c, 0)
     back = lax.dot_general(dy_rows, w_out, T_DIMS, preferred_element_type=f32)
-    back = back.reshape(-1, 2 * rows, width)[:, :rows].reshape(tokens)
     q, k, v = (a.reshape(tokens) for a in (queries, keys, values))
+    cfg = jnp.concatenate([reg, steps[0].astype(f32)]).reshape(1, -1)
     pre = exchange(scan(exchange(own), False))
 
     sol, dual, mixed, grad_q, send = call(
         solve_kernel,
         [(tokens, f32), (tokens, f32), (tokens, bf16), (tokens, bf16), (packed, bf16)],
-        2,
-        5,
+        0,
+        6,
         [
             pltpu.VMEM((2, 256, 128), f32),
             pltpu.VMEM((2, 256, 128), f32),
@@ -250,7 +270,7 @@
             pltpu.VMEM((2, 256, 128), bf16),
         ],
         flops=2 * 10**9,
-    )(steps, reg, q, k, v, back, pre)
+    )(cfg, q, k, v, back, pre)
     out = lax.psum_scatter(
         jnp.dot(mixed, w_out, preferred_element_type=f32).astype(bf16),
         "head",
@@ -268,24 +288,26 @@
 
 
 def solution(mesh):
+    spans, groups = mesh.devices.shape
+    apart = Mesh(mesh.devices.reshape(spans // 2, 2, groups), SEQ + ("head",))
     placed = (
-        P("seq", "head", None),
-        P("seq", "head", None),
-        P("seq", "head", None),
+        P(SEQ, "head", None),
+        P(SEQ, "head", None),
+        P(SEQ, "head", None),
         P("head"),
-        P("seq", "head"),
+        P(SEQ, "head"),
         P("head", None),
-        P(("seq", "head"), None),
+        P(SEQ + ("head",), None),
     )
     return jax.shard_map(
         local,
-        mesh=mesh,
+        mesh=apart,
         in_specs=placed,
         out_specs=(
-            P(("seq", "head"), None),
-            P("seq", "head", None),
-            P("seq", "head", None),
-            P("seq", "head", None),
+            P(SEQ + ("head",), None),
+            P(SEQ, "head", None),
+            P(SEQ, "head", None),
+            P(SEQ, "head", None),
         ),
         check_vma=False,
     )

time: 134 us -> 135 us (level); the launches traced: 132 us -> 134 us
  Pallas kernels: 7.55 us -> 16.5 us
  blocking collectives: 28.7 us -> 24.8 us
  other arithmetic: 1.6 us -> 0.08 us
    pallas_call x1, Pallas kernels: 2.97 us -> 11.3 us  [local(): call(solve_kernel, [(tokens, f32), (tokens, f32), (tokens, bf16), (tokens...]
    all_to_all x3, waiting for transfers between devices: 36.5 us -> 30 us  [exchange(): moved = lax.all_to_all(parts.reshape(spans, 2, -1), SEQ, 0, 0)]
    all_gather x1, waiting for transfers between devices: 4.39 us -> 9.56 us  [local(): dy_rows = lax.all_gather(d_y, ('core', 'head'), axis=0, tiled=True)]
    all_to_all x1, blocking collectives: 28.7 us -> 24.8 us  [exchange(): moved = lax.all_to_all(parts.reshape(spans, 2, -1), SEQ, 0, 0)]
    concatenate x1 -> x0, other arithmetic: 1.6 us -> none  [local(): jnp.concatenate([d_y, d_y], axis=0)]
  transfers between devices with their start and end apart: 5 -> 5, of which waited for: 4 -> 4; matrix products, arithmetic and copies ran while one was open for 2% -> 2% of each run, Pallas kernels for 3% -> 4%
where the time goes in v3:
time: 135 us; the launch traced here: 134 us
  waiting for transfers between devices  40.2 us (30%)
  starting transfers between devices  33.9 us (25%)
  blocking collectives  24.8 us (18%)
  Pallas kernels  16.5 us (12%)
  between operations  14.2 us (11%)
  matrix products  2.64 us (2%)
  local copies, waits for them, and re-layouts  2.02 us (1%)
    all_to_all x3, starting transfers between devices, exchange(): moved = lax.all_to_all(parts.reshape(spans, 2, -1), SEQ, 0, 0)  33.6 us
    all_to_all x3, waiting for transfers between devices, exchange(): moved = lax.all_to_all(parts.reshape(spans, 2, -1), SEQ, 0, 0)  30 us
    all_to_all x1, blocking collectives, exchange(): moved = lax.all_to_all(parts.reshape(spans, 2, -1), SEQ, 0, 0)  24.8 us
    pallas_call x1, Pallas kernels, local(): call(solve_kernel, [(tokens, f32), (tokens, f32), (tokens, bf16), (tokens...  11.3 us
    all_gather x1, waiting for transfers between devices, local(): dy_rows = lax.all_gather(d_y, ('core', 'head'), axis=0, tiled=True)  9.56 us
  transfers between devices with their start and end apart: 5, of which 4 were waited for; matrix products, arithmetic and copies ran while one was open for 2% of the time, Pallas kernels for 4%

profile of v3, /device:TPU:1, one launch (start us, length us, event | category | flops | bytes accessed | tf_op | source)
XLA Modules:
  0.0 134.3 jit_solution(1955955591503632918)
XLA Ops:
  7.2 0.0 copy-start
  7.2 0.0 all-gather.2.cloned.1.call-start
  7.2 0.7 all-gather.2.cloned.1.call-update
  7.9 1.8 %shard_map.102 = bf16[576,128]{1,0:T(8,128)(2,1)} custom-call(bf16[256,128]{1,0:T(8,128)(2,1)} %bitcast.64, bf16[256,128]{1,0:T(8,128)(2,1)} %bitcast.61), custom_call_target="tpu_custom_call" | custom-call | tf_op jit(solution)/shard_map/pallas_call | solution.py:252
  9.7 0.0 copy-start.3
  9.7 20.2 %all-to-all-start = ((bf16[96,2,384]{2,1,0:T(2,128)(2,1)}), bf16[96,2,384]{2,1,0:T(2,128)(2,1)S(1)}, u32[]{:S(2)}, u32[]{:S(2)}) async-start(bf16[96,2,384]{2,1,0:T(2,128)(2,1)} %bitcast.73), calls=%async_computation | async-start | bytes 294912 | tf_op jit(solution)/shard_map/all_to_all | solution.py:244
  29.9 0.0 copy-done.3
  29.9 0.0 copy-start.4
  29.9 0.6 copy-done.4
  30.6 0.0 copy-start.5
  30.6 0.7 copy-done.5
  31.2 0.1 maximum_bitcast_fusion.cfg_ref
  31.3 13.2 %all-to-all-done = bf16[96,2,384]{2,1,0:T(2,128)(2,1)S(1)} async-done(((bf16[96,2,384]{2,1,0:T(2,128)(2,1)}), bf16[96,2,384]{2,1,0:T(2,128)(2,1)S(1)}, u32[]{:S(2)}, u32[]{:S(2)}) %all-to-all-start) | async-done | bytes 147488 | tf_op jit(solution)/shard_map/all_to_all | solution.py:244
  44.5 0.9 shard_map.103
  45.4 0.0 copy-start.1
  45.4 0.0 copy-start.2
  45.4 6.8 %all-to-all-start.1 = ((bf16[96,2,384]{2,1,0:T(2,128)(2,1)}), bf16[96,2,384]{2,1,0:T(2,128)(2,1)S(1)}, u32[]{:S(2)}, u32[]{:S(2)}) async-start(bf16[96,2,384]{2,1,0:T(2,128)(2,1)} %bitcast.12), calls=%async_computation.1 | async-start | bytes 294912 | tf_op jit(solution)/shard_map/all_to_all | solution.py:244
  52.2 0.2 reduce-scatter.2.cloned.1.call-start
  52.5 0.0 copy-done.1
  52.5 0.0 copy-done.2
  52.5 9.6 %all-gather.2.cloned.1.call-done = bf16[256,2048]{1,0:T(8,128)(2,1)} async-done(((bf16[16,2048]{1,0:T(8,128)(2,1)}), bf16[256,2048]{1,0:T(8,128)(2,1)}) %all-gather.2.cloned.1.call-update) | async-done | bytes 1048592 | tf_op jit(solution)/shard_map/all_gather | solution.py:253
  62.1 0.0 copy-done
  62.1 1.5 %fusion.back_ref = f32[128,256]{1,0:T(8,128)S(1)} fusion(bf16[256,2048]{1,0:T(8,128)(2,1)S(1)} %copy-done, bf16[256,2048]{1,0:T(8,128)(2,1)} %all-gather.2.cloned.1.call-done, s32[]{:T(128)S(6)} %select_n.3), kind=kOutput, calls=%fused_computation.1 | convolution fusion | flops 134217728 | bytes 1703940 | tf_op jit(solution)/shard_map/dot_general | solution.py:255
  63.6 3.4 %all-to-all-done.1 = bf16[96,2,384]{2,1,0:T(2,128)(2,1)S(1)} async-done(((bf16[96,2,384]{2,1,0:T(2,128)(2,1)}), bf16[96,2,384]{2,1,0:T(2,128)(2,1)S(1)}, u32[]{:S(2)}, u32[]{:S(2)}) %all-to-all-start.1) | async-done | bytes 147488 | tf_op jit(solution)/shard_map/all_to_all | solution.py:244
  67.0 11.3 %shard_map.104 = (f32[128,256]{1,0:T(8,128)S(1)}, f32[128,256]{1,0:T(8,128)S(1)}, bf16[128,256]{1,0:T(8,128)(2,1)S(1)}, bf16[128,256]{1,0:T(8,128)(2,1)S(1)}, bf16[576,128]{1,0:T(8,128)(2,1)S(1)}) custom-call(f32[1,4]{1,0:T(1,128)S(1)} %maximum_bitcast_fusion.cfg_ref, bf16[128,256]{1,0:T(8,128)(2,1)S(1)} %bitcast.72, ...), custom_call_target="tpu_custom_call" | custom-call | flops 2000000000 | tf_op jit(solution)/shard_map/pallas_call | solution.py:260
  78.3 1.1 convolution_convert_fusion
  79.4 0.0 reduce-scatter.2.cloned.1.call-update
  79.4 24.8 %all_to_all.20 = bf16[96,2,384]{2,1,0:T(2,128)(2,1)S(1)} all-to-all(bf16[96,2,384]{2,1,0:T(2,128)(2,1)S(1)} %bitcast.71), channel_id=1, replica_groups=mesh['chip'=48,'core'=2,'head'=8] {'chip','core'}, dimensions={0} | all-to-all | bytes 294912 | tf_op jit(solution)/shard_map/all_to_all | solution.py:244
  104.3 0.9 shard_map.106
  105.2 6.7 %all-to-all-start.3 = ((bf16[96,2,384]{2,1,0:T(2,128)(2,1)}), bf16[96,2,384]{2,1,0:T(2,128)(2,1)S(1)}, u32[]{:S(2)}, u32[]{:S(2)}) async-start(bf16[96,2,384]{2,1,0:T(2,128)(2,1)} %bitcast.24), calls=%async_computation.4 | async-start | bytes 294912 | tf_op jit(solution)/shard_map/all_to_all | solution.py:244
  111.8 0.6 shard_map.105
  112.5 0.7 reshape.98
  113.1 13.4 %all-to-all-done.3 = bf16[96,2,384]{2,1,0:T(2,128)(2,1)S(1)} async-done(((bf16[96,2,384]{2,1,0:T(2,128)(2,1)}), bf16[96,2,384]{2,1,0:T(2,128)(2,1)S(1)}, u32[]{:S(2)}, u32[]{:S(2)}) %all-to-all-start.3) | async-done | bytes 147488 | tf_op jit(solution)/shard_map/all_to_all | solution.py:244
  126.6 0.9 shard_map.107
  127.5 0.0 reduce-scatter.2.cloned.1.call-done
  (5 shorter events, 0.1 us)
Async XLA Ops:
  7.2 54.9 %copy-start = (bf16[256,2048]{1,0:T(8,128)(2,1)S(1)}, bf16[256,2048]{1,0:T(8,128)(2,1)}, u32[]{:S(2)}) copy-start(bf16[256,2048]{1,0:T(8,128)(2,1)} %param.12) | copy-start | bytes 3145732
  7.2 54.9 %all-gather.2.cloned.1.call-start = ((), (), s32[]{:S(2)}) async-start(), calls=%async_computation.5 | async-start | bytes 1114112 | tf_op jit(solution)/shard_map/all_gather | solution.py:253
  9.7 20.2 %copy-start.3 = (bf16[128,2,128]{2,1,0:T(2,128)(2,1)S(1)}, bf16[128,2,128]{2,1,0:T(2,128)(2,1)}, u32[]{:S(2)}) copy-start(bf16[128,2,128]{2,1,0:T(2,128)(2,1)} %param.7) | copy-start | bytes 196612
  9.7 34.8 %all-to-all-start = ((bf16[96,2,384]{2,1,0:T(2,128)(2,1)}), bf16[96,2,384]{2,1,0:T(2,128)(2,1)S(1)}, u32[]{:S(2)}, u32[]{:S(2)}) async-start(bf16[96,2,384]{2,1,0:T(2,128)(2,1)} %bitcast.73), calls=%async_computation | async-start | bytes 294912 | tf_op jit(solution)/shard_map/all_to_all | solution.py:244
  29.9 0.7 copy-start.4
  30.6 0.7 copy-start.5
  45.4 7.0 %copy-start.1 = (bf16[128,2,128]{2,1,0:T(2,128)(2,1)S(1)}, bf16[128,2,128]{2,1,0:T(2,128)(2,1)}, u32[]{:S(2)}) copy-start(bf16[128,2,128]{2,1,0:T(2,128)(2,1)} %param.9) | copy-start | bytes 196612
  45.4 7.0 %copy-start.2 = (bf16[128,2,128]{2,1,0:T(2,128)(2,1)S(1)}, bf16[128,2,128]{2,1,0:T(2,128)(2,1)}, u32[]{:S(2)}) copy-start(bf16[128,2,128]{2,1,0:T(2,128)(2,1)} %param.8) | copy-start | bytes 196612
  45.4 21.5 %all-to-all-start.1 = ((bf16[96,2,384]{2,1,0:T(2,128)(2,1)}), bf16[96,2,384]{2,1,0:T(2,128)(2,1)S(1)}, u32[]{:S(2)}, u32[]{:S(2)}) async-start(bf16[96,2,384]{2,1,0:T(2,128)(2,1)} %bitcast.12), calls=%async_computation.1 | async-start | bytes 294912 | tf_op jit(solution)/shard_map/all_to_all | solution.py:244
  52.2 75.2 %reduce-scatter.2.cloned.1.call-start = ((), (), s32[]{:S(2)}) async-start(), calls=%async_computation.6 | async-start | bytes 589824 | tf_op jit(solution)/shard_map/reduce_scatter | solution.py:274
  105.2 21.4 %all-to-all-start.3 = ((bf16[96,2,384]{2,1,0:T(2,128)(2,1)}), bf16[96,2,384]{2,1,0:T(2,128)(2,1)S(1)}, u32[]{:S(2)}, u32[]{:S(2)}) async-start(bf16[96,2,384]{2,1,0:T(2,128)(2,1)} %bitcast.24), calls=%async_computation.4 | async-start | bytes 294912 | tf_op jit(solution)/shard_map/all_to_all | solution.py:244
Sparse Core Ops, SparseCore 0:
  10.4 51.5 all-gather.1
  79.6 33.3 reduce-scatter.1

commit v4 on v3

--- a/solution.py
+++ b/solution.py
@@ -123,7 +123,7 @@
     low = causal(128)
     low_two = causal(256)
     ridges = [jnp.broadcast_to(cfg_ref[:, h : h + 1], (1, 128)) for h in range(2)]
-    counts = [cfg_ref[:, 2 + h : 3 + h] for h in range(2)]
+    counts = [jnp.broadcast_to(cfg_ref[:, 2 + h : 3 + h], (1, 128)) for h in range(2)]
     rrs = []
     for h in range(2):
         lanes = slice(h * 128, (h + 1) * 128)
@@ -149,8 +149,8 @@
         images = [firsts[h][:, :128] + seconds[h] + ridges[h] * ps[h] for h in range(2)]
         alphas = [rrs[h] / (jnp.sum(ps[h] * images[h], -1, keepdims=True) + epsilon) for h in range(2)]
         for h in range(2):
-            kept = jnp.where(i < counts[h], alphas[h], 0.0)
-            x_s[h] = x_s[h] + kept * ps[h]
+            live = jnp.where(i < counts[h], 1.0, 0.0)
+            x_s[h] = x_s[h] + alphas[h] * (ps[h] * live)
             if i == STEPS_MAX - 1:
                 continue
             r = r_s[h] - alphas[h] * images[h]

time: 135 us -> 130 us (0.963)
  Pallas kernels: 16.5 us -> 11.9 us
    pallas_call x1, Pallas kernels: 11.3 us -> 6.79 us  [local(): call(solve_kernel, [(tokens, f32), (tokens, f32), (tokens, bf16), (tokens...]
where the time goes in v4:
time: 130 us
  waiting for transfers between devices  40.4 us (31%)
  starting transfers between devices  33.7 us (26%)
  blocking collectives  24.8 us (19%)
  between operations  14.2 us (11%)
  Pallas kernels  11.9 us (9%)
  matrix products  2.64 us (2%)
  local copies, waits for them, and re-layouts  2.02 us (2%)
    all_to_all x3, starting transfers between devices, exchange(): moved = lax.all_to_all(parts.reshape(spans, 2, -1), SEQ, 0, 0)  33.6 us
    all_to_all x3, waiting for transfers between devices, exchange(): moved = lax.all_to_all(parts.reshape(spans, 2, -1), SEQ, 0, 0)  30 us
    all_to_all x1, blocking collectives, exchange(): moved = lax.all_to_all(parts.reshape(spans, 2, -1), SEQ, 0, 0)  24.8 us
    all_gather x1, waiting for transfers between devices, local(): dy_rows = lax.all_gather(d_y, ('core', 'head'), axis=0, tiled=True)  9.74 us
    pallas_call x1, Pallas kernels, local(): call(solve_kernel, [(tokens, f32), (tokens, f32), (tokens, bf16), (tokens...  6.79 us
  transfers between devices with their start and end apart: 5, of which 4 were waited for; matrix products, arithmetic and copies ran while one was open for 2% of the time, Pallas kernels for 4%

profile of v4, /device:TPU:1, one launch (start us, length us, event | category | flops | bytes accessed | tf_op | source)
XLA Modules:
  0.0 129.7 jit_solution(5981983657422739768)
XLA Ops:
  7.2 0.0 copy-start
  7.2 0.0 all-gather.2.cloned.1.call-start
  7.2 0.7 all-gather.2.cloned.1.call-update
  7.9 1.8 %shard_map.102 = bf16[576,128]{1,0:T(8,128)(2,1)} custom-call(bf16[256,128]{1,0:T(8,128)(2,1)} %bitcast.64, bf16[256,128]{1,0:T(8,128)(2,1)} %bitcast.61), custom_call_target="tpu_custom_call" | custom-call | tf_op jit(solution)/shard_map/pallas_call | solution.py:252
  9.7 0.0 copy-start.3
  9.7 20.2 %all-to-all-start = ((bf16[96,2,384]{2,1,0:T(2,128)(2,1)}), bf16[96,2,384]{2,1,0:T(2,128)(2,1)S(1)}, u32[]{:S(2)}, u32[]{:S(2)}) async-start(bf16[96,2,384]{2,1,0:T(2,128)(2,1)} %bitcast.73), calls=%async_computation | async-start | bytes 294912 | tf_op jit(solution)/shard_map/all_to_all | solution.py:244
  29.9 0.0 copy-done.3
  29.9 0.0 copy-start.4
  29.9 0.6 copy-done.4
  30.6 0.0 copy-start.5
  30.6 0.7 copy-done.5
  31.2 0.1 maximum_bitcast_fusion.cfg_ref
  31.3 13.2 %all-to-all-done = bf16[96,2,384]{2,1,0:T(2,128)(2,1)S(1)} async-done(((bf16[96,2,384]{2,1,0:T(2,128)(2,1)}), bf16[96,2,384]{2,1,0:T(2,128)(2,1)S(1)}, u32[]{:S(2)}, u32[]{:S(2)}) %all-to-all-start) | async-done | bytes 147488 | tf_op jit(solution)/shard_map/all_to_all | solution.py:244
  44.5 0.9 shard_map.103
  45.4 0.0 copy-start.1
  45.4 0.0 copy-start.2
  45.4 6.8 %all-to-all-start.1 = ((bf16[96,2,384]{2,1,0:T(2,128)(2,1)}), bf16[96,2,384]{2,1,0:T(2,128)(2,1)S(1)}, u32[]{:S(2)}, u32[]{:S(2)}) async-start(bf16[96,2,384]{2,1,0:T(2,128)(2,1)} %bitcast.12), calls=%async_computation.1 | async-start | bytes 294912 | tf_op jit(solution)/shard_map/all_to_all | solution.py:244
  52.2 0.0 reduce-scatter.2.cloned.1.call-start
  52.3 0.0 copy-done.1
  52.3 0.0 copy-done.2
  52.3 9.7 %all-gather.2.cloned.1.call-done = bf16[256,2048]{1,0:T(8,128)(2,1)} async-done(((bf16[16,2048]{1,0:T(8,128)(2,1)}), bf16[256,2048]{1,0:T(8,128)(2,1)}) %all-gather.2.cloned.1.call-update) | async-done | bytes 1048592 | tf_op jit(solution)/shard_map/all_gather | solution.py:253
  62.1 0.0 copy-done
  62.1 1.5 %fusion.back_ref = f32[128,256]{1,0:T(8,128)S(1)} fusion(bf16[256,2048]{1,0:T(8,128)(2,1)S(1)} %copy-done, bf16[256,2048]{1,0:T(8,128)(2,1)} %all-gather.2.cloned.1.call-done, s32[]{:T(128)S(6)} %select_n.3), kind=kOutput, calls=%fused_computation.1 | convolution fusion | flops 134217728 | bytes 1703940 | tf_op jit(solution)/shard_map/dot_general | solution.py:255
  63.6 3.4 %all-to-all-done.1 = bf16[96,2,384]{2,1,0:T(2,128)(2,1)S(1)} async-done(((bf16[96,2,384]{2,1,0:T(2,128)(2,1)}), bf16[96,2,384]{2,1,0:T(2,128)(2,1)S(1)}, u32[]{:S(2)}, u32[]{:S(2)}) %all-to-all-start.1) | async-done | bytes 147488 | tf_op jit(solution)/shard_map/all_to_all | solution.py:244
  67.0 6.8 %shard_map.104 = (f32[128,256]{1,0:T(8,128)S(1)}, f32[128,256]{1,0:T(8,128)S(1)}, bf16[128,256]{1,0:T(8,128)(2,1)S(1)}, bf16[128,256]{1,0:T(8,128)(2,1)S(1)}, bf16[576,128]{1,0:T(8,128)(2,1)S(1)}) custom-call(f32[1,4]{1,0:T(1,128)S(1)} %maximum_bitcast_fusion.cfg_ref, bf16[128,256]{1,0:T(8,128)(2,1)S(1)} %bitcast.72, ...), custom_call_target="tpu_custom_call" | custom-call | flops 2000000000 | tf_op jit(solution)/shard_map/pallas_call | solution.py:260
  73.7 1.1 convolution_convert_fusion
  74.9 0.0 reduce-scatter.2.cloned.1.call-update
  74.9 24.8 %all_to_all.20 = bf16[96,2,384]{2,1,0:T(2,128)(2,1)S(1)} all-to-all(bf16[96,2,384]{2,1,0:T(2,128)(2,1)S(1)} %bitcast.71), channel_id=1, replica_groups=mesh['chip'=48,'core'=2,'head'=8] {'chip','core'}, dimensions={0} | all-to-all | bytes 294912 | tf_op jit(solution)/shard_map/all_to_all | solution.py:244
  99.7 0.9 shard_map.106
  100.6 6.7 %all-to-all-start.3 = ((bf16[96,2,384]{2,1,0:T(2,128)(2,1)}), bf16[96,2,384]{2,1,0:T(2,128)(2,1)S(1)}, u32[]{:S(2)}, u32[]{:S(2)}) async-start(bf16[96,2,384]{2,1,0:T(2,128)(2,1)} %bitcast.24), calls=%async_computation.4 | async-start | bytes 294912 | tf_op jit(solution)/shard_map/all_to_all | solution.py:244
  107.3 0.6 shard_map.105
  107.9 0.7 reshape.98
  108.6 13.4 %all-to-all-done.3 = bf16[96,2,384]{2,1,0:T(2,128)(2,1)S(1)} async-done(((bf16[96,2,384]{2,1,0:T(2,128)(2,1)}), bf16[96,2,384]{2,1,0:T(2,128)(2,1)S(1)}, u32[]{:S(2)}, u32[]{:S(2)}) %all-to-all-start.3) | async-done | bytes 147488 | tf_op jit(solution)/shard_map/all_to_all | solution.py:244
  122.0 0.9 shard_map.107
  122.9 0.0 reduce-scatter.2.cloned.1.call-done
  (5 shorter events, 0.1 us)
Async XLA Ops:
  7.2 54.9 %copy-start = (bf16[256,2048]{1,0:T(8,128)(2,1)S(1)}, bf16[256,2048]{1,0:T(8,128)(2,1)}, u32[]{:S(2)}) copy-start(bf16[256,2048]{1,0:T(8,128)(2,1)} %param.12) | copy-start | bytes 3145732
  7.2 54.9 %all-gather.2.cloned.1.call-start = ((), (), s32[]{:S(2)}) async-start(), calls=%async_computation.5 | async-start | bytes 1114112 | tf_op jit(solution)/shard_map/all_gather | solution.py:253
  9.7 20.2 %copy-start.3 = (bf16[128,2,128]{2,1,0:T(2,128)(2,1)S(1)}, bf16[128,2,128]{2,1,0:T(2,128)(2,1)}, u32[]{:S(2)}) copy-start(bf16[128,2,128]{2,1,0:T(2,128)(2,1)} %param.7) | copy-start | bytes 196612
  9.7 34.8 %all-to-all-start = ((bf16[96,2,384]{2,1,0:T(2,128)(2,1)}), bf16[96,2,384]{2,1,0:T(2,128)(2,1)S(1)}, u32[]{:S(2)}, u32[]{:S(2)}) async-start(bf16[96,2,384]{2,1,0:T(2,128)(2,1)} %bitcast.73), calls=%async_computation | async-start | bytes 294912 | tf_op jit(solution)/shard_map/all_to_all | solution.py:244
  29.9 0.7 copy-start.4
  30.6 0.7 copy-start.5
  45.4 6.9 %copy-start.1 = (bf16[128,2,128]{2,1,0:T(2,128)(2,1)S(1)}, bf16[128,2,128]{2,1,0:T(2,128)(2,1)}, u32[]{:S(2)}) copy-start(bf16[128,2,128]{2,1,0:T(2,128)(2,1)} %param.9) | copy-start | bytes 196612
  45.4 6.9 %copy-start.2 = (bf16[128,2,128]{2,1,0:T(2,128)(2,1)S(1)}, bf16[128,2,128]{2,1,0:T(2,128)(2,1)}, u32[]{:S(2)}) copy-start(bf16[128,2,128]{2,1,0:T(2,128)(2,1)} %param.8) | copy-start | bytes 196612
  45.4 21.5 %all-to-all-start.1 = ((bf16[96,2,384]{2,1,0:T(2,128)(2,1)}), bf16[96,2,384]{2,1,0:T(2,128)(2,1)S(1)}, u32[]{:S(2)}, u32[]{:S(2)}) async-start(bf16[96,2,384]{2,1,0:T(2,128)(2,1)} %bitcast.12), calls=%async_computation.1 | async-start | bytes 294912 | tf_op jit(solution)/shard_map/all_to_all | solution.py:244
  52.2 70.7 %reduce-scatter.2.cloned.1.call-start = ((), (), s32[]{:S(2)}) async-start(), calls=%async_computation.6 | async-start | bytes 589824 | tf_op jit(solution)/shard_map/reduce_scatter | solution.py:274
  100.6 21.4 %all-to-all-start.3 = ((bf16[96,2,384]{2,1,0:T(2,128)(2,1)}), bf16[96,2,384]{2,1,0:T(2,128)(2,1)S(1)}, u32[]{:S(2)}, u32[]{:S(2)}) async-start(bf16[96,2,384]{2,1,0:T(2,128)(2,1)} %bitcast.24), calls=%async_computation.4 | async-start | bytes 294912 | tf_op jit(solution)/shard_map/all_to_all | solution.py:244
Sparse Core Ops, SparseCore 0:
  10.4 51.5 all-gather.1
  75.0 33.3 reduce-scatter.1

commit v5 on v4

--- a/solution.py
+++ b/solution.py
@@ -108,10 +108,10 @@
     v_ref,
     back_ref,
     pre_ref,
+    w_ref,
     sol_ref,
     dual_ref,
-    mixed_ref,
-    grad_q_ref,
+    part_ref,
     send_ref,
     x_s,
     r_s,
@@ -159,7 +159,7 @@
             p_s[h] = r + (new / (rrs[h] + epsilon)) * ps[h]
             rrs[h] = new
 
-    syms, crosses = [], []
+    syms, crosses, mixes = [], [], []
     for h in range(2):
         lanes = slice(h * 128, (h + 1) * 128)
         k, v, back = k_ref[:, lanes], v_ref[:, lanes], back_ref[:, lanes]
@@ -167,11 +167,10 @@
         sol, dual = x_s[h, :128, :], x_s[h, 128:, :]
         sol_ref[:, lanes] = sol
         dual_ref[:, lanes] = dual
-        grad_q_ref[:, lanes] = dual.astype(bf16)
         firsts = wide(sol)
         scores = jnp.where(low, dot(firsts, jnp.concatenate([k, k], axis=1), T_DIMS), 0.0)
         mixed = dot(firsts, jnp.concatenate([state, state], axis=1), T_DIMS) + dot(wide(scores), twice(v))
-        mixed_ref[:, lanes] = mixed.astype(bf16)
+        mixes.append(mixed.astype(bf16))
         sol_high, sol_low = halves(sol)
         dual_high, dual_low = halves(dual)
         back_high, back_low = halves(back)
@@ -189,32 +188,44 @@
             )
         )
     pack(syms + crosses, send_ref)
-
-
-def inner_kernel(k_ref, v_ref, back_ref, sol_ref, dual_ref, gk_ref, gv_ref):
+    mixes = jnp.concatenate(mixes, axis=1)
+    for g in range(w_ref.shape[1] // 256):
+        lanes = slice(g * 256, (g + 1) * 256)
+        part_ref[:, lanes] = dot(mixes, w_ref[:, lanes]).astype(bf16)
+
+
+def alternate(both):
+    r = lax.broadcasted_iota(jnp.int32, (256, 256), 0)
+    c = lax.broadcasted_iota(jnp.int32, (256, 256), 1)
+    source = (r & 1) * 128 + lax.shift_right_logical(r, 1)
+    return dot(jnp.where(c == source, 1.0, 0.0).astype(bf16), both).astype(bf16)
+
+
+def final_kernel(
+    k_ref, v_ref, back_ref, sol_ref, dual_ref, suf_ref, grad_q_ref, grad_k_ref, grad_v_ref
+):
+    mats = unpack(suf_ref)
     up = causal(128, True)
+    grads = []
     for h in range(2):
         lanes = slice(h * 128, (h + 1) * 128)
         k, v, back = k_ref[:, lanes], v_ref[:, lanes], back_ref[:, lanes]
         sol, dual = sol_ref[:, lanes], dual_ref[:, lanes]
+        sym, cross = mats[h], mats[2 + h]
         kk = jnp.concatenate([k, k], axis=1)
         vv = jnp.concatenate([v, v], axis=1)
         one = wide(jnp.where(up, dot(kk, wide(sol), T_DIMS), 0.0))
         two = wide(jnp.where(up, dot(kk, wide(dual), T_DIMS), 0.0))
         three = wide(jnp.where(up, dot(vv, wide(back), T_DIMS), 0.0))
         sol_b, dual_b, back_b = sol.astype(bf16), dual.astype(bf16), back.astype(bf16)
-        gk_ref[:, lanes] = dot(three, twice(sol_b)) - dot(one, twice(dual_b)) - dot(two, twice(sol_b))
-        gv_ref[:, lanes] = dot(one, twice(back_b))
-
-
-def final_kernel(k_ref, v_ref, gk_ref, gv_ref, suf_ref, grad_k_ref, grad_v_ref):
-    sym0, sym1, cross0, cross1 = unpack(suf_ref)
-    k, v = heads_apart(k_ref[...]), heads_apart(v_ref[...])
-    cross = jnp.concatenate([cross0, cross1], axis=0)
-    sym = jnp.concatenate([sym0, sym1], axis=0)
-    cross_lanes = jnp.concatenate([cross0, cross1], axis=1)
-    grad_k_ref[...] = (gk_ref[...] + dot(v, cross) - dot(k, sym)).astype(bf16)
-    grad_v_ref[...] = (gv_ref[...] + dot(k, cross_lanes, T_DIMS)).astype(bf16)
+        grad_k = dot(three, twice(sol_b)) - dot(one, twice(dual_b)) - dot(two, twice(sol_b))
+        grad_k = grad_k + dot(v, cross) - dot(k, sym)
+        grad_v = dot(one, twice(back_b)) + dot(k, cross, T_DIMS)
+        grads.append(jnp.concatenate([dual_b, grad_k.astype(bf16), grad_v.astype(bf16)], axis=1))
+    both = alternate(jnp.concatenate(grads, axis=0))
+    grad_q_ref[...] = both[:, :128]
+    grad_k_ref[...] = both[:, 128:256]
+    grad_v_ref[...] = both[:, 256:]
 
 
 def call(kernel, outs, n_smem=0, n_in=0, scratch=(), flops=0, bytes_accessed=0, vmem=24):
@@ -257,11 +268,11 @@
     cfg = jnp.concatenate([reg, steps[0].astype(f32)]).reshape(1, -1)
     pre = exchange(scan(exchange(own), False))
 
-    sol, dual, mixed, grad_q, send = call(
+    sol, dual, part, send = call(
         solve_kernel,
-        [(tokens, f32), (tokens, f32), (tokens, bf16), (tokens, bf16), (packed, bf16)],
+        [(tokens, f32), (tokens, f32), ((size_c, w_out.shape[1]), bf16), (packed, bf16)],
         0,
-        6,
+        7,
         [
             pltpu.VMEM((2, 256, 128), f32),
             pltpu.VMEM((2, 256, 128), f32),
@@ -270,19 +281,11 @@
             pltpu.VMEM((2, 256, 128), bf16),
         ],
         flops=2 * 10**9,
-    )(cfg, q, k, v, back, pre)
-    out = lax.psum_scatter(
-        jnp.dot(mixed, w_out, preferred_element_type=f32).astype(bf16),
-        "head",
-        scatter_dimension=0,
-        tiled=True,
-    )
+    )(cfg, q, k, v, back, pre, w_out)
+    out = lax.psum_scatter(part, "head", scatter_dimension=0, tiled=True)
     suf = exchange(scan(exchange(send), True))
-    gk, gv = call(inner_kernel, [(tokens, f32), (tokens, f32)], 0, 5, flops=2 * 10**8)(
-        k, v, back, sol, dual
-    )
-    grad_k, grad_v = call(final_kernel, [(pairs, bf16), (pairs, bf16)], 0, 5)(
-        k_pairs, v_pairs, gk.reshape(heads).reshape(pairs), gv.reshape(heads).reshape(pairs), suf
+    grad_q, grad_k, grad_v = call(final_kernel, [(pairs, bf16)] * 3, 0, 6)(
+        k, v, back, sol, dual, suf
     )
     return out, grad_q.reshape(heads), grad_k.reshape(heads), grad_v.reshape(heads)
 

time: 130 us -> 129 us (level)
  blocking collectives: 24.8 us -> 45.8 us
  waiting for transfers between devices: 40.4 us -> 26.2 us
  starting transfers between devices: 33.7 us -> 26.9 us
  other arithmetic: 0.08 us -> 1.39 us
    all_to_all x1 -> x2, blocking collectives: 24.8 us -> 45.8 us  [exchange(): moved = lax.all_to_all(parts.reshape(spans, 2, -1), SEQ, 0, 0)]
    all_to_all x3 -> x2, waiting for transfers between devices: 30 us -> 15.6 us  [exchange(): moved = lax.all_to_all(parts.reshape(spans, 2, -1), SEQ, 0, 0)]
    all_to_all x3 -> x2, starting transfers between devices: 33.6 us -> 26.8 us  [exchange(): moved = lax.all_to_all(parts.reshape(spans, 2, -1), SEQ, 0, 0)]
    pallas_call x3 -> x2, Pallas kernels: 8.33 us -> 9.31 us  [the longest x1 7.73 us: local(): call(solve_kernel, [(tokens, f32), (tokens, f32), ((size_c, w_out.shape[1...]
  transfers between devices with their start and end apart: 5 -> 4, of which waited for: 4 -> 3; matrix products, arithmetic and copies ran while one was open for 2% -> 3% of each run, Pallas kernels for 4% -> 3%
where the time goes in v5:
time: 129 us
  blocking collectives  45.8 us (36%)
  starting transfers between devices  26.9 us (21%)
  waiting for transfers between devices  26.2 us (20%)
  between operations  14.1 us (11%)
  Pallas kernels  12.2 us (9%)
  matrix products  1.53 us (1%)
  other arithmetic  1.39 us (1%)
    all_to_all x2, blocking collectives, exchange(): moved = lax.all_to_all(parts.reshape(spans, 2, -1), SEQ, 0, 0)  45.8 us
    all_to_all x2, starting transfers between devices, exchange(): moved = lax.all_to_all(parts.reshape(spans, 2, -1), SEQ, 0, 0)  26.8 us
    all_to_all x2, waiting for transfers between devices, exchange(): moved = lax.all_to_all(parts.reshape(spans, 2, -1), SEQ, 0, 0)  15.6 us
    all_gather x1, waiting for transfers between devices, local(): dy_rows = lax.all_gather(d_y, ('core', 'head'), axis=0, tiled=True)  9.88 us
    pallas_call x1, Pallas kernels, local(): call(solve_kernel, [(tokens, f32), (tokens, f32), ((size_c, w_out.shape[1...  7.73 us
  transfers between devices with their start and end apart: 4, of which 3 were waited for; matrix products, arithmetic and copies ran while one was open for 3% of the time, Pallas kernels for 3%

profile of v5, /device:TPU:1, one launch (start us, length us, event | category | flops | bytes accessed | tf_op | source)
XLA Modules:
  0.0 129.0 jit_solution(10699115088034553545)
XLA Ops:
  7.2 0.0 copy-start
  7.2 0.0 all-gather.2.cloned.1.call-start
  7.2 0.7 all-gather.2.cloned.1.call-update
  7.9 1.8 %shard_map.102 = bf16[576,128]{1,0:T(8,128)(2,1)} custom-call(bf16[256,128]{1,0:T(8,128)(2,1)} %bitcast.70, bf16[256,128]{1,0:T(8,128)(2,1)} %bitcast.68), custom_call_target="tpu_custom_call" | custom-call | tf_op jit(solution)/shard_map/pallas_call | solution.py:263
  9.7 20.0 %all-to-all-start = ((bf16[96,2,384]{2,1,0:T(2,128)(2,1)}), bf16[96,2,384]{2,1,0:T(2,128)(2,1)S(1)}, u32[]{:S(2)}, u32[]{:S(2)}) async-start(bf16[96,2,384]{2,1,0:T(2,128)(2,1)} %bitcast.67), calls=%async_computation | async-start | bytes 294912 | tf_op jit(solution)/shard_map/all_to_all | solution.py:255
  29.8 0.9 copy.17
  30.6 0.7 convert_bitcast_fusion
  31.3 0.7 maximum_bitcast_fusion.cfg_ref
  32.0 12.4 %all-to-all-done = bf16[96,2,384]{2,1,0:T(2,128)(2,1)S(1)} async-done(((bf16[96,2,384]{2,1,0:T(2,128)(2,1)}), bf16[96,2,384]{2,1,0:T(2,128)(2,1)S(1)}, u32[]{:S(2)}, u32[]{:S(2)}) %all-to-all-start) | async-done | bytes 147488 | tf_op jit(solution)/shard_map/all_to_all | solution.py:255
  44.4 0.9 shard_map.103
  45.3 0.0 copy-start.1
  45.3 0.0 copy-start.2
  45.3 6.8 %all-to-all-start.1 = ((bf16[96,2,384]{2,1,0:T(2,128)(2,1)}), bf16[96,2,384]{2,1,0:T(2,128)(2,1)S(1)}, u32[]{:S(2)}, u32[]{:S(2)}) async-start(bf16[96,2,384]{2,1,0:T(2,128)(2,1)} %bitcast.12), calls=%async_computation.1 | async-start | bytes 294912 | tf_op jit(solution)/shard_map/all_to_all | solution.py:255
  52.1 0.0 reduce-scatter.2.cloned.1.call-start
  52.1 0.0 copy-done.1
  52.1 0.0 copy-done.2
  52.2 9.9 %all-gather.2.cloned.1.call-done = bf16[256,2048]{1,0:T(8,128)(2,1)} async-done(((bf16[16,2048]{1,0:T(8,128)(2,1)}), bf16[256,2048]{1,0:T(8,128)(2,1)}) %all-gather.2.cloned.1.call-update) | async-done | bytes 1048592 | tf_op jit(solution)/shard_map/all_gather | solution.py:264
  62.0 0.0 copy-done
  62.1 1.5 %fusion.back_ref = f32[128,256]{1,0:T(8,128)S(1)} fusion(bf16[256,2048]{1,0:T(8,128)(2,1)S(1)} %copy-done, bf16[256,2048]{1,0:T(8,128)(2,1)} %all-gather.2.cloned.1.call-done, s32[]{:T(128)S(6)} %select_n.3), kind=kOutput, calls=%fused_computation | convolution fusion | flops 134217728 | bytes 1703940 | tf_op jit(solution)/shard_map/dot_general | solution.py:266
  63.6 3.2 %all-to-all-done.1 = bf16[96,2,384]{2,1,0:T(2,128)(2,1)S(1)} async-done(((bf16[96,2,384]{2,1,0:T(2,128)(2,1)}), bf16[96,2,384]{2,1,0:T(2,128)(2,1)S(1)}, u32[]{:S(2)}, u32[]{:S(2)}) %all-to-all-start.1) | async-done | bytes 147488 | tf_op jit(solution)/shard_map/all_to_all | solution.py:255
  66.8 7.7 %shard_map.104 = (f32[128,256]{1,0:T(8,128)S(1)}, f32[128,256]{1,0:T(8,128)S(1)}, bf16[128,2048]{1,0:T(8,128)(2,1)}, bf16[576,128]{1,0:T(8,128)(2,1)S(1)}) custom-call(f32[1,4]{1,0:T(1,128)S(1)} %maximum_bitcast_fusion.cfg_ref, bf16[128,256]{1,0:T(8,128)(2,1)S(1)} %bitcast.66, bf16[128,256]{1,0:T(8,128)(2,1)S(1)} %get-tuple-element.19.k_ref, ...), custom_call_target="tpu_custom_call" | custom-call | flops 2000000000 | tf_op jit(solution)/shard_map/pallas_call | solution.py:271
  74.5 0.0 reduce-scatter.2.cloned.1.call-update
  74.6 25.0 %all_to_all.20 = bf16[96,2,384]{2,1,0:T(2,128)(2,1)S(1)} all-to-all(bf16[96,2,384]{2,1,0:T(2,128)(2,1)S(1)} %bitcast.65), channel_id=1, replica_groups=mesh['chip'=48,'core'=2,'head'=8] {'chip','core'}, dimensions={0} | all-to-all | bytes 294912 | tf_op jit(solution)/shard_map/all_to_all | solution.py:255
  99.5 0.2 shard_map.105
  99.8 20.8 %all_to_all.21 = bf16[96,2,384]{2,1,0:T(2,128)(2,1)S(1)} all-to-all(bf16[96,2,384]{2,1,0:T(2,128)(2,1)S(1)} %bitcast.62), channel_id=1, replica_groups=mesh['chip'=48,'core'=2,'head'=8] {'chip','core'}, dimensions={0} | all-to-all | bytes 294912 | tf_op jit(solution)/shard_map/all_to_all | solution.py:255
  120.5 1.6 %shard_map.106 = (bf16[256,128]{1,0:T(8,128)(2,1)}, bf16[256,128]{1,0:T(8,128)(2,1)}, bf16[256,128]{1,0:T(8,128)(2,1)}) custom-call(bf16[128,256]{1,0:T(8,128)(2,1)S(1)} %get-tuple-element.19.k_ref, bf16[128,256]{1,0:T(8,128)(2,1)S(1)} %get-tuple-element.18.v_ref, f32[128,256]{1,0:T(8,128)S(1)} %fusion.back_ref, f32[128,256]{1,0:T(8,128)S(1)} %get-tuple-element.12.sol_ref, ...), custom_call_target="tpu_custom_call" | custom-call | tf_op jit(solution)/shard_map/pallas_call | solution.py:287
  122.1 0.0 reduce-scatter.2.cloned.1.call-done
  (1 shorter events, 0.0 us)
Async XLA Ops:
  7.2 54.9 %copy-start = (bf16[256,2048]{1,0:T(8,128)(2,1)S(1)}, bf16[256,2048]{1,0:T(8,128)(2,1)}, u32[]{:S(2)}) copy-start(bf16[256,2048]{1,0:T(8,128)(2,1)} %w_ref.1) | copy-start | bytes 3145732
  7.2 54.9 %all-gather.2.cloned.1.call-start = ((), (), s32[]{:S(2)}) async-start(), calls=%async_computation.5 | async-start | bytes 1114112 | tf_op jit(solution)/shard_map/all_gather | solution.py:264
  9.7 34.7 %all-to-all-start = ((bf16[96,2,384]{2,1,0:T(2,128)(2,1)}), bf16[96,2,384]{2,1,0:T(2,128)(2,1)S(1)}, u32[]{:S(2)}, u32[]{:S(2)}) async-start(bf16[96,2,384]{2,1,0:T(2,128)(2,1)} %bitcast.67), calls=%async_computation | async-start | bytes 294912 | tf_op jit(solution)/shard_map/all_to_all | solution.py:255
  45.3 6.9 %copy-start.1 = (bf16[128,2,128]{2,1,0:T(2,128)(2,1)S(1)}, bf16[128,2,128]{2,1,0:T(2,128)(2,1)}, u32[]{:S(2)}) copy-start(bf16[128,2,128]{2,1,0:T(2,128)(2,1)} %param.9) | copy-start | bytes 196612
  45.3 6.9 %copy-start.2 = (bf16[128,2,128]{2,1,0:T(2,128)(2,1)S(1)}, bf16[128,2,128]{2,1,0:T(2,128)(2,1)}, u32[]{:S(2)}) copy-start(bf16[128,2,128]{2,1,0:T(2,128)(2,1)} %param.8) | copy-start | bytes 196612
  45.3 21.5 %all-to-all-start.1 = ((bf16[96,2,384]{2,1,0:T(2,128)(2,1)}), bf16[96,2,384]{2,1,0:T(2,128)(2,1)S(1)}, u32[]{:S(2)}, u32[]{:S(2)}) async-start(bf16[96,2,384]{2,1,0:T(2,128)(2,1)} %bitcast.12), calls=%async_computation.1 | async-start | bytes 294912 | tf_op jit(solution)/shard_map/all_to_all | solution.py:255
  52.1 70.1 %reduce-scatter.2.cloned.1.call-start = ((), (), s32[]{:S(2)}) async-start(), calls=%async_computation.6 | async-start | bytes 589824 | tf_op jit(solution)/shard_map/reduce_scatter | solution.py:285
Sparse Core Ops, SparseCore 0:
  10.4 51.5 all-gather.1
  74.7 33.5 reduce-scatter.1

commit v6 on v5

--- a/solution.py
+++ b/solution.py
@@ -106,35 +106,48 @@
     q_ref,
     k_ref,
     v_ref,
-    back_ref,
+    rows_ref,
     pre_ref,
     w_ref,
     sol_ref,
     dual_ref,
     part_ref,
     send_ref,
+    back_ref,
     x_s,
     r_s,
     p_s,
     b_s,
     k_s,
+    rows_s,
+    w_s,
+    sem,
 ):
+    size = rows_s.shape[0]
+    first_row = pl.multiple_of(lax.axis_index("core") * size, size)
+    fetch = pltpu.make_async_copy(rows_ref.at[pl.ds(first_row, size), :], rows_s, sem.at[0])
+    fetch_w = pltpu.make_async_copy(w_ref, w_s, sem.at[1])
+    fetch.start()
+    fetch_w.start()
     mats = unpack(pre_ref)
     low = causal(128)
     low_two = causal(256)
     ridges = [jnp.broadcast_to(cfg_ref[:, h : h + 1], (1, 128)) for h in range(2)]
     counts = [jnp.broadcast_to(cfg_ref[:, 2 + h : 3 + h], (1, 128)) for h in range(2)]
+    for h in range(2):
+        k = k_ref[:, h * 128 : (h + 1) * 128]
+        b_s[h] = twice(jnp.concatenate([mats[h], k.T], axis=1))
+        k_s[h] = twice(k)
+    fetch.wait()
+    fetch_w.wait()
+    back_ref[...] = dot(rows_s[...], w_s[...], T_DIMS)
     rrs = []
     for h in range(2):
         lanes = slice(h * 128, (h + 1) * 128)
         k, v, back = k_ref[:, lanes], v_ref[:, lanes], back_ref[:, lanes]
-        cov, state = mats[h], mats[2 + h]
-        both = jnp.concatenate([cov, k.T], axis=1)
-        b_s[h] = twice(both)
-        k_s[h] = twice(k)
         firsts = wide(back)
         scores = jnp.where(low, dot(firsts, jnp.concatenate([v, v], axis=1), T_DIMS), 0.0)
-        adjoint = dot(firsts, twice(state)) + dot(wide(scores), twice(k))
+        adjoint = dot(firsts, twice(mats[2 + h])) + dot(wide(scores), twice(k))
         right = jnp.concatenate([q_ref[:, lanes].astype(f32), adjoint], axis=0)
         x_s[h] = jnp.zeros_like(right)
         r_s[h] = right
@@ -191,7 +204,7 @@
     mixes = jnp.concatenate(mixes, axis=1)
     for g in range(w_ref.shape[1] // 256):
         lanes = slice(g * 256, (g + 1) * 256)
-        part_ref[:, lanes] = dot(mixes, w_ref[:, lanes]).astype(bf16)
+        part_ref[:, lanes] = dot(mixes, w_s[:, lanes]).astype(bf16)
 
 
 def alternate(both):
@@ -228,12 +241,14 @@
     grad_v_ref[...] = both[:, 256:]
 
 
-def call(kernel, outs, n_smem=0, n_in=0, scratch=(), flops=0, bytes_accessed=0, vmem=24):
+def call(kernel, outs, n_smem=0, n_in=0, scratch=(), flops=0, bytes_accessed=0, vmem=24, hbm=()):
+    specs = [pl.BlockSpec(memory_space=pltpu.SMEM)] * n_smem + [pl.BlockSpec(memory_space=pltpu.VMEM)] * n_in
+    for i in hbm:
+        specs[i] = pl.BlockSpec(memory_space=pltpu.HBM)
     return pl.pallas_call(
         kernel,
         out_shape=[jax.ShapeDtypeStruct(s, d) for s, d in outs],
-        in_specs=[pl.BlockSpec(memory_space=pltpu.SMEM)] * n_smem
-        + [pl.BlockSpec(memory_space=pltpu.VMEM)] * n_in,
+        in_specs=specs,
         out_specs=[pl.BlockSpec(memory_space=pltpu.VMEM)] * len(outs),
         scratch_shapes=list(scratch),
         compiler_params=pltpu.CompilerParams(vmem_limit_bytes=vmem * 1024 * 1024),
@@ -262,15 +277,13 @@
     k_pairs, v_pairs = keys.reshape(pairs), values.reshape(pairs)
     (own,) = call(own_kernel, [(packed, bf16)], 0, 2, vmem=56)(k_pairs, v_pairs)
     dy_rows = lax.all_gather(d_y, ("core", "head"), axis=0, tiled=True)
-    dy_rows = lax.dynamic_slice_in_dim(dy_rows, lax.axis_index("core") * size_c, size_c, 0)
-    back = lax.dot_general(dy_rows, w_out, T_DIMS, preferred_element_type=f32)
     q, k, v = (a.reshape(tokens) for a in (queries, keys, values))
     cfg = jnp.concatenate([reg, steps[0].astype(f32)]).reshape(1, -1)
     pre = exchange(scan(exchange(own), False))
 
-    sol, dual, part, send = call(
+    sol, dual, part, send, back = call(
         solve_kernel,
-        [(tokens, f32), (tokens, f32), ((size_c, w_out.shape[1]), bf16), (packed, bf16)],
+        [(tokens, f32), (tokens, f32), ((size_c, w_out.shape[1]), bf16), (packed, bf16), (tokens, f32)],
         0,
         7,
         [
@@ -279,9 +292,14 @@
             pltpu.VMEM((2, 256, 128), f32),
             pltpu.VMEM((2, 256, 256), bf16),
             pltpu.VMEM((2, 256, 128), bf16),
+            pltpu.VMEM((size_c, w_out.shape[1]), bf16),
+            pltpu.VMEM(w_out.shape, bf16),
+            pltpu.SemaphoreType.DMA((2,)),
         ],
+        hbm=(4, 6),
+        vmem=53,
         flops=2 * 10**9,
-    )(cfg, q, k, v, back, pre, w_out)
+    )(cfg, q, k, v, dy_rows, pre, w_out)
     out = lax.psum_scatter(part, "head", scatter_dimension=0, tiled=True)
     suf = exchange(scan(exchange(send), True))
     grad_q, grad_k, grad_v = call(final_kernel, [(pairs, bf16)] * 3, 0, 6)(

time: 129 us -> 130 us (level)
  blocking collectives: 45.8 us -> 78.9 us
  starting transfers between devices: 26.9 us -> 6.88 us
  waiting for transfers between devices: 26.2 us -> 14.5 us
  Pallas kernels: 12.2 us -> 14.4 us
  matrix products: 1.53 us -> 0 us
  other arithmetic: 1.39 us -> 0.08 us
    all_to_all x2 -> x3, blocking collectives: 45.8 us -> 78.9 us  [exchange(): moved = lax.all_to_all(parts.reshape(spans, 2, -1), SEQ, 0, 0)]
    all_to_all x2 -> x1, starting transfers between devices: 26.8 us -> 6.8 us  [exchange(): moved = lax.all_to_all(parts.reshape(spans, 2, -1), SEQ, 0, 0)]
    all_gather x1, waiting for transfers between devices: 9.88 us -> 0.01 us  [local(): dy_rows = lax.all_gather(d_y, ('core', 'head'), axis=0, tiled=True)]
    pallas_call x1, Pallas kernels: 7.73 us -> 9.92 us  [local(): call(solve_kernel, [(tokens, f32), (tokens, f32), ((size_c, w_out.shape[1...]
    all_to_all x2 -> x1, waiting for transfers between devices: 15.6 us -> 13.8 us  [exchange(): moved = lax.all_to_all(parts.reshape(spans, 2, -1), SEQ, 0, 0)]
    dot_general x1 -> x0, matrix products: 1.53 us -> none  [local(): back = lax.dot_general(dy_rows, w_out, T_DIMS, preferred_element_type=f32)]
  transfers between devices with their start and end apart: 4 -> 3, of which waited for: 3 -> 1; matrix products, arithmetic and copies ran while one was open for 3% -> 0% of each run, Pallas kernels for 3% -> 3%
where the time goes in v6:
time: 130 us
  blocking collectives  78.9 us (61%)
  waiting for transfers between devices  14.5 us (11%)
  Pallas kernels  14.4 us (11%)
  between operations  14.1 us (11%)
  starting transfers between devices  6.88 us (5%)
    all_to_all x3, blocking collectives, exchange(): moved = lax.all_to_all(parts.reshape(spans, 2, -1), SEQ, 0, 0)  78.9 us
    all_to_all x1, waiting for transfers between devices, exchange(): moved = lax.all_to_all(parts.reshape(spans, 2, -1), SEQ, 0, 0)  13.8 us
    pallas_call x1, Pallas kernels, local(): call(solve_kernel, [(tokens, f32), (tokens, f32), ((size_c, w_out.shape[1...  9.92 us
    all_to_all x1, starting transfers between devices, exchange(): moved = lax.all_to_all(parts.reshape(spans, 2, -1), SEQ, 0, 0)  6.8 us
  transfers between devices with their start and end apart: 3, of which 1 were waited for; matrix products, arithmetic and copies ran while one was open for 0% of the time, Pallas kernels for 3%

profile of v6, /device:TPU:1, one launch (start us, length us, event | category | flops | bytes accessed | tf_op | source)
XLA Modules:
  0.0 129.6 jit_solution(7806598620275006685)
XLA Ops:
  7.2 0.0 all-gather.2.cloned.1.call-start
  7.2 0.7 all-gather.2.cloned.1.call-update
  7.9 1.8 %shard_map.102 = bf16[576,128]{1,0:T(8,128)(2,1)} custom-call(bf16[256,128]{1,0:T(8,128)(2,1)} %bitcast.69, bf16[256,128]{1,0:T(8,128)(2,1)} %bitcast.67), custom_call_target="tpu_custom_call" | custom-call | tf_op jit(solution)/shard_map/pallas_call | solution.py:278
  9.7 34.6 %all_to_all.20 = bf16[96,2,384]{2,1,0:T(2,128)(2,1)S(1)} all-to-all(bf16[96,2,384]{2,1,0:T(2,128)(2,1)} %bitcast.66), channel_id=1, replica_groups=mesh['chip'=48,'core'=2,'head'=8] {'chip','core'}, dimensions={0} | all-to-all | bytes 294912 | tf_op jit(solution)/shard_map/all_to_all | solution.py:270
  44.4 0.9 shard_map.103
  45.2 0.0 copy-start.3
  45.2 0.0 copy-start.2
  45.2 0.0 copy-start.4
  45.2 6.8 %all-to-all-start.1 = ((bf16[96,2,384]{2,1,0:T(2,128)(2,1)}), bf16[96,2,384]{2,1,0:T(2,128)(2,1)S(1)}, u32[]{:S(2)}, u32[]{:S(2)}) async-start(bf16[96,2,384]{2,1,0:T(2,128)(2,1)} %bitcast.12), calls=%async_computation.1 | async-start | bytes 294912 | tf_op jit(solution)/shard_map/all_to_all | solution.py:270
  52.1 0.0 reduce-scatter.2.cloned.1.call-start
  52.1 0.0 copy-done.3
  52.1 0.0 copy-done.2
  52.1 0.0 copy-start
  52.1 0.0 copy-start.1
  52.2 0.0 copy-done.4
  52.2 0.1 maximum_bitcast_fusion.cfg_ref
  52.3 0.7 copy-done
  53.0 0.0 copy-done.1
  53.0 13.8 %all-to-all-done.1 = bf16[96,2,384]{2,1,0:T(2,128)(2,1)S(1)} async-done(((bf16[96,2,384]{2,1,0:T(2,128)(2,1)}), bf16[96,2,384]{2,1,0:T(2,128)(2,1)S(1)}, u32[]{:S(2)}, u32[]{:S(2)}) %all-to-all-start.1) | async-done | bytes 147488 | tf_op jit(solution)/shard_map/all_to_all | solution.py:270
  66.8 0.0 all-gather.2.cloned.1.call-done.rows_ref
  66.8 9.9 %shard_map.104 = (f32[128,256]{1,0:T(8,128)S(1)}, f32[128,256]{1,0:T(8,128)S(1)}, bf16[128,2048]{1,0:T(8,128)(2,1)}, bf16[576,128]{1,0:T(8,128)(2,1)S(1)}, f32[128,256]{1,0:T(8,128)S(1)}) custom-call(f32[1,4]{1,0:T(1,128)S(1)} %maximum_bitcast_fusion.cfg_ref, bf16[128,256]{1,0:T(8,128)(2,1)S(1)} %bitcast.65, bf16[128,256]{1,0:T(8,128)(2,1)S(1)} %get-tuple-element.21.k_ref, ...), custom_call_target="tpu_custom_call" | custom-call | flops 2000000000 | tf_op jit(solution)/shard_map/pallas_call | solution.py:284
  76.7 0.0 reduce-scatter.2.cloned.1.call-update
  76.7 23.4 %all_to_all.21 = bf16[96,2,384]{2,1,0:T(2,128)(2,1)S(1)} all-to-all(bf16[96,2,384]{2,1,0:T(2,128)(2,1)S(1)} %bitcast.64), channel_id=1, replica_groups=mesh['chip'=48,'core'=2,'head'=8] {'chip','core'}, dimensions={0} | all-to-all | bytes 294912 | tf_op jit(solution)/shard_map/all_to_all | solution.py:270
  100.2 0.2 shard_map.105
  100.4 20.8 %all_to_all.22 = bf16[96,2,384]{2,1,0:T(2,128)(2,1)S(1)} all-to-all(bf16[96,2,384]{2,1,0:T(2,128)(2,1)S(1)} %bitcast.61), channel_id=1, replica_groups=mesh['chip'=48,'core'=2,'head'=8] {'chip','core'}, dimensions={0} | all-to-all | bytes 294912 | tf_op jit(solution)/shard_map/all_to_all | solution.py:270
  121.2 1.6 %shard_map.106 = (bf16[256,128]{1,0:T(8,128)(2,1)}, bf16[256,128]{1,0:T(8,128)(2,1)}, bf16[256,128]{1,0:T(8,128)(2,1)}) custom-call(bf16[128,256]{1,0:T(8,128)(2,1)S(1)} %get-tuple-element.21.k_ref, bf16[128,256]{1,0:T(8,128)(2,1)S(1)} %get-tuple-element.20.v_ref, f32[128,256]{1,0:T(8,128)S(1)} %get-tuple-element.13.back_ref, ...), custom_call_target="tpu_custom_call" | custom-call | tf_op jit(solution)/shard_map/pallas_call | solution.py:305
  122.8 0.0 reduce-scatter.2.cloned.1.call-done
  (3 shorter events, 0.0 us)
Async XLA Ops:
  7.2 59.6 %all-gather.2.cloned.1.call-start = ((), (), s32[]{:S(2)}) async-start(), calls=%async_computation.5 | async-start | bytes 1114112 | tf_op jit(solution)/shard_map/all_gather | solution.py:279
  45.2 6.9 %copy-start.3 = (s32[1,2]{1,0:T(1,128)S(1)}, s32[1,2]{1,0:T(1,128)}, u32[]{:S(2)}) copy-start(s32[1,2]{1,0:T(1,128)} %param.11) | copy-start | bytes 28
  45.2 6.9 %copy-start.2 = (bf16[128,2,128]{2,1,0:T(2,128)(2,1)S(1)}, bf16[128,2,128]{2,1,0:T(2,128)(2,1)}, u32[]{:S(2)}) copy-start(bf16[128,2,128]{2,1,0:T(2,128)(2,1)} %param.7) | copy-start | bytes 196612
  45.2 6.9 %copy-start.4 = (f32[2]{0:T(128)S(1)}, f32[2]{0:T(128)}, u32[]{:S(2)}) copy-start(f32[2]{0:T(128)} %param.10) | copy-start | bytes 28
  45.2 21.5 %all-to-all-start.1 = ((bf16[96,2,384]{2,1,0:T(2,128)(2,1)}), bf16[96,2,384]{2,1,0:T(2,128)(2,1)S(1)}, u32[]{:S(2)}, u32[]{:S(2)}) async-start(bf16[96,2,384]{2,1,0:T(2,128)(2,1)} %bitcast.12), calls=%async_computation.1 | async-start | bytes 294912 | tf_op jit(solution)/shard_map/all_to_all | solution.py:270
  52.1 70.7 %reduce-scatter.2.cloned.1.call-start = ((), (), s32[]{:S(2)}) async-start(), calls=%async_computation.6 | async-start | bytes 589824 | tf_op jit(solution)/shard_map/reduce_scatter | solution.py:303
  52.1 0.8 copy-start
  52.1 0.9 copy-start.1
Sparse Core Ops, SparseCore 0:
  10.4 51.5 all-gather.1
  76.9 31.9 reduce-scatter.1
